TPU v7x, 128 devices: a whole 4x4x4 slice. The times are simulated.
128 devices in a mesh: row: 8 (over x_lo, y), col: 16 (over x_hi, z, core).
Axes of the slice: x: 4 (x_hi: 2, x_lo: 2; x = x_hi * 2 + x_lo), y: 4, z: 4, core: 2. Of those that a mesh axis runs over, the one named last changes fastest.
Arguments:
- blocks: bfloat16 [8, 16, 24, 256, 256], P('row', 'col'), may hold values from 0.049804688 to 1
- block_rows: int32 [8, 16, 24], P('row', 'col'), may hold values from 0 to 255, as said below
- block_cols: int32 [8, 16, 24], P('row', 'col'), may hold values from 0 to 255
- live_count: int32 [8, 16], P('row', 'col'), may hold values from 6 to 24, as said below
- slab: bfloat16 [65536, 2048], P(('row', 'col')), may hold values from 0.0099487305 to 1
Outputs:
- inflated: float32 [65536, 2048], P(('row', 'col'))
Inputs may be any that keep to these rules, and one draw needn't show every extreme that they name: For tile (i, j) the 24 slots name distinct block positions; block_rows lie in i * 32 to (i + 1) * 32 - 1, and block_cols are among the numbers ((c // 2) * 16 + j) * 2 + c % 2 for c in 0 to 15. `live_count`: some tile is full and some tile holds the fewest.
All inputs are finite; a program needn't handle non-finite values.
Results may differ from a plain program's by a relative error of at most 0.0003.
Values may be sent and summed in bfloat16 or wider, within the bound.
A program may use at most 320 MiB of HBM per device.

v0:
```python
import jax
import jax.numpy as jnp
from jax import lax
from jax.sharding import PartitionSpec as P

slot_group = 8


def body(blocks, block_rows, block_cols, live_count, slab):
    col_count = lax.axis_size("col")
    row_count = lax.axis_size("row")
    block_size = blocks.shape[-1]
    slab_width = slab.shape[1]
    per_device = slab.shape[0] // block_size
    tile_height = per_device * col_count
    tile_breadth = per_device * row_count
    slot_total = blocks.shape[2]
    tile_blocks = blocks.reshape(slot_total, block_size, block_size)
    rows_local = block_rows.reshape(slot_total) - lax.axis_index("row") * tile_height
    cols_global = block_cols.reshape(slot_total)
    cols_local = cols_global // per_device // col_count * per_device + cols_global % per_device
    live_slots = live_count.reshape(())
    gathered = lax.all_gather(slab, "row", axis=0, tiled=True)
    slab_table = gathered.reshape(tile_breadth, block_size, slab_width)

    def add_group(group, partial_value):
        offset = group * slot_group
        chosen = lax.dynamic_slice_in_dim(tile_blocks, offset, slot_group, 0)
        row_index = lax.dynamic_slice_in_dim(rows_local, offset, slot_group, 0)
        col_index = lax.dynamic_slice_in_dim(cols_local, offset, slot_group, 0)
        pieces = slab_table[col_index]
        product = jnp.einsum("sab,sbk->sak", chosen, pieces, preferred_element_type=jnp.float32)
        in_use = (offset + jnp.arange(slot_group) < live_slots).astype(jnp.float32)
        return partial_value.at[row_index].add(product * in_use[:, None, None])

    partial_value = jnp.zeros((tile_height, block_size, slab_width), jnp.float32)
    partial_value = lax.fori_loop(0, slot_total // slot_group, add_group, partial_value)
    partial_value = partial_value.reshape(tile_height * block_size, slab_width)
    proteins = tile_height * block_size * row_count
    expanded = lax.psum_scatter(partial_value, "col", scatter_dimension=0, tiled=True)
    square = expanded * expanded
    column_mass = lax.psum(jnp.sum(square, axis=0), ("row", "col"))
    return proteins * square / column_mass


def solution(mesh):
    placed = (
        P("row", "col", None, None, None),
        P("row", "col", None),
        P("row", "col", None),
        P("row", "col"),
        P(("row", "col"), None),
    )
    return jax.shard_map(
        body, mesh=mesh, in_specs=placed, out_specs=P(("row", "col"), None), check_vma=False
    )
```

profile of v0, /device:TPU:1, one launch (start us, length us, event | category | flops | bytes accessed | tf_op | source)
XLA Modules:
  0.0 895.9 jit_solution(2017811338184336032)
XLA Ops:
  6.5 0.7 all-gather.2.cloned.1.call-update
  7.3 0.7 fusion.2
  8.0 0.7 subtract_bitcast_fusion
  8.6 174.1 %all-gather.2.cloned.1.call-done = bf16[4096,2048]{1,0:T(8,128)(2,1)} async-done(((bf16[512,2048]{1,0:T(8,128)(2,1)}), bf16[4096,2048]{1,0:T(8,128)(2,1)}) %all-gather.2.cloned.1.call-update) | async-done | bytes 16777232 | tf_op jit(solution)/shard_map/all_gather | solution.py:23
  182.8 21.2 %broadcast_in_dim.21 = f32[32,256,2048]{2,1,0:T(8,128)} broadcast(f32[]{:T(128)} %constant.83.clone.1), dimensions={} | broadcast | bytes 67108864 | tf_op jit(solution)/shard_map/broadcast_in_dim | solution.py:36
  204.0 161.4 %while.13 = (s32[]{:T(128)}, f32[32,256,2048]{2,1,0:T(8,128)}, s32[24]{0:T(128)S(1)}, bf16[24,256,256]{2,1,0:T(8,128)(2,1)}, s32[24]{0:T(128)S(1)}, /*index=5*/b...) while((s32[]{:T(128)}, f32[32,256,2048]{2,1,0:T(8,128)}, ...), condition=%wide.region_2.3_spmd, body=%wide.region_0.2_spmd.sunk | while | flops 2155873280 | bytes 93327816 | solution.py:37
  204.0 0.6 compare_convert_fusion.2
  204.7 0.1 compare_select_fusion.9
  204.7 10.5 %gather_fusion = bf16[8,256,2048]{2,1,0:T(8,128)(2,1)} fusion(bf16[16,256,2048]{2,1,0:T(8,128)(2,1)} %get-tuple-element.220, s32[1024]{0:T(1024)S(1)} %pad_clamp_fusion.2), kind=kCustom, calls=%fused_computation.clone.1 | custom fusion | bytes 16777248 | tf_op jit(solution)/shard_map/while/body/eval_jaxpr/gather | solution.py:31
  215.3 11.9 %broadcast_multiply_fusion.2 = f32[8,256,2048]{2,1,0:T(8,128)} fusion(f32[8]{0:T(128)S(1)} %compare_convert_fusion.2, bf16[8,256,2048]{2,1,0:T(8,128)(2,1)} %gather_fusion, bf16[24,256,256]{2,1,0:T(8,128)(2,1)} %get-tuple-element.218, s32[]{:T(128)S(6)} %select_n.55), kind=kOutput, calls=%fused_computation.2.clone.1 | convolution fusion | flops 2151677952 | bytes 26214436 | tf_op jit(solution)/shard_map/while/body/eval_jaxpr/sab,sbk->sak/dot_general | solution.py:32
  227.1 30.8 %scatter_fusion = f32[32,256,2048]{2,1,0:T(8,128)} fusion(f32[32,256,2048]{2,1,0:T(8,128)} %get-tuple-element.205, s32[8]{0:T(128)S(1)} %get-tuple-element.191, f32[8,256,2048]{2,1,0:T(8,128)} %broadcast_multiply_fusion.2), kind=kCustom, calls=%fused_computation.1.clone.1 | custom fusion | flops 4194304 | bytes 50331680 | tf_op jit(solution)/shard_map/while/body/eval_jaxpr/scatter-add | solution.py:34
  257.9 0.6 compare_convert_fusion.2
  258.6 0.1 compare_select_fusion.9
  258.7 10.5 %gather_fusion = bf16[8,256,2048]{2,1,0:T(8,128)(2,1)} fusion(bf16[16,256,2048]{2,1,0:T(8,128)(2,1)} %get-tuple-element.220, s32[1024]{0:T(1024)S(1)} %pad_clamp_fusion.2), kind=kCustom, calls=%fused_computation.clone.1 | custom fusion | bytes 16777248 | tf_op jit(solution)/shard_map/while/body/eval_jaxpr/gather | solution.py:31
  269.2 11.9 %broadcast_multiply_fusion.2 = f32[8,256,2048]{2,1,0:T(8,128)} fusion(f32[8]{0:T(128)S(1)} %compare_convert_fusion.2, bf16[8,256,2048]{2,1,0:T(8,128)(2,1)} %gather_fusion, bf16[24,256,256]{2,1,0:T(8,128)(2,1)} %get-tuple-element.218, s32[]{:T(128)S(6)} %select_n.55), kind=kOutput, calls=%fused_computation.2.clone.1 | convolution fusion | flops 2151677952 | bytes 26214436 | tf_op jit(solution)/shard_map/while/body/eval_jaxpr/sab,sbk->sak/dot_general | solution.py:32
  281.1 30.7 %scatter_fusion = f32[32,256,2048]{2,1,0:T(8,128)} fusion(f32[32,256,2048]{2,1,0:T(8,128)} %get-tuple-element.205, s32[8]{0:T(128)S(1)} %get-tuple-element.191, f32[8,256,2048]{2,1,0:T(8,128)} %broadcast_multiply_fusion.2), kind=kCustom, calls=%fused_computation.1.clone.1 | custom fusion | flops 4194304 | bytes 50331680 | tf_op jit(solution)/shard_map/while/body/eval_jaxpr/scatter-add | solution.py:34
  311.7 0.6 compare_convert_fusion.2
  312.5 10.5 %gather_fusion = bf16[8,256,2048]{2,1,0:T(8,128)(2,1)} fusion(bf16[16,256,2048]{2,1,0:T(8,128)(2,1)} %get-tuple-element.220, s32[1024]{0:T(1024)S(1)} %pad_clamp_fusion.2), kind=kCustom, calls=%fused_computation.clone.1 | custom fusion | bytes 16777248 | tf_op jit(solution)/shard_map/while/body/eval_jaxpr/gather | solution.py:31
  323.0 11.9 %broadcast_multiply_fusion.2 = f32[8,256,2048]{2,1,0:T(8,128)} fusion(f32[8]{0:T(128)S(1)} %compare_convert_fusion.2, bf16[8,256,2048]{2,1,0:T(8,128)(2,1)} %gather_fusion, bf16[24,256,256]{2,1,0:T(8,128)(2,1)} %get-tuple-element.218, s32[]{:T(128)S(6)} %select_n.55), kind=kOutput, calls=%fused_computation.2.clone.1 | convolution fusion | flops 2151677952 | bytes 26214436 | tf_op jit(solution)/shard_map/while/body/eval_jaxpr/sab,sbk->sak/dot_general | solution.py:32
  334.9 30.6 %scatter_fusion = f32[32,256,2048]{2,1,0:T(8,128)} fusion(f32[32,256,2048]{2,1,0:T(8,128)} %get-tuple-element.205, s32[8]{0:T(128)S(1)} %get-tuple-element.191, f32[8,256,2048]{2,1,0:T(8,128)} %broadcast_multiply_fusion.2), kind=kCustom, calls=%fused_computation.1.clone.1 | custom fusion | flops 4194304 | bytes 50331680 | tf_op jit(solution)/shard_map/while/body/eval_jaxpr/scatter-add | solution.py:34
  365.5 450.1 %reduce-scatter.2.cloned.1.call-done = f32[512,2048]{1,0:T(8,128)} async-done(((f32[8192,2048]{1,0:T(8,128)}), f32[512,2048]{1,0:T(8,128)}) %reduce-scatter.2.cloned.1.call-update) | async-done | bytes 4194320 | tf_op jit(solution)/shard_map/reduce_scatter | solution.py:40
  815.6 2.6 multiply_reduce_fusion
  818.1 65.9 %psum.7 = f32[2048]{0:T(1024)S(1)} all-reduce(f32[2048]{0:T(1024)S(1)} %multiply_reduce_fusion), channel_id=1, replica_groups=mesh['row'=8,'col'=16] {'row','col'}, use_global_device_ids=true, to_apply=%region_5.6 | all-reduce | flops 2048 | bytes 16384 | tf_op jit(solution)/shard_map/psum | solution.py:42
  884.1 5.0 multiply_divide_fusion
  (7 shorter events, 0.2 us)
Async XLA Ops:
  6.5 176.2 %all-gather.2.cloned.1.call-start = ((), (), s32[]{:S(2)}) async-start(), calls=%async_computation.1 | async-start | bytes 18874368 | tf_op jit(solution)/shard_map/all_gather | solution.py:23
  7.3 808.3 %reduce-scatter.2.cloned.1.call-start = ((), (), s32[]{:S(2)}) async-start(), calls=%async_computation.2 | async-start | bytes 71303168 | tf_op jit(solution)/shard_map/reduce_scatter | solution.py:40
Sparse Core Ops, SparseCore 0:
  9.0 173.7 all-gather.1
  365.6 449.9 reduce-scatter.1
where the time goes:
time: 896 us
  waiting for transfers between devices  625 us (70%)
  other arithmetic  103 us (11%)
  blocking collectives  65.9 us (7%)
  local copies, waits for them, and re-layouts  52.8 us (6%)
  matrix products  35.6 us (4%)
  between operations  13.4 us (1%)
    reduce_scatter x1, waiting for transfers between devices, body(): lax.psum_scatter(partial_value, 'col', scatter_dimension=0, tiled=True)  450 us
    all_gather x1, waiting for transfers between devices, body(): gathered = lax.all_gather(slab, 'row', axis=0, tiled=True)  174 us
    scatter-add x3, other arithmetic, add_group(): return partial_value.at[row_index].add(product * in_use[:, None, None])  92.1 us
    psum x1, blocking collectives, body(): column_mass = lax.psum(jnp.sum(square, axis=0), ('row', 'col'))  65.9 us
    dot_general x3, matrix products, add_group(): jnp.einsum('sab,sbk->sak', chosen, pieces, preferred_element_type=jnp.flo...  35.6 us
    gather x3, local copies, waits for them, and re-layouts, add_group(): pieces = slab_table[col_index]  31.6 us
    broadcast_in_dim x1, local copies, waits for them, and re-layouts, body(): jnp.zeros((tile_height, block_size, slab_width), jnp.float32)  21.2 us
  transfers between devices with their start and end apart: 2, of which 2 were waited for; matrix products, arithmetic and copies ran while one was open for 0% of the time, Pallas kernels for 0%

commit v1 on v0

v1 whole, which is shorter than its diff:
```python
import functools

import jax
import jax.numpy as jnp
from jax import lax
from jax.experimental import pallas as pl
from jax.experimental.pallas import tpu as pltpu
from jax.sharding import PartitionSpec as P

MESH = pl.DeviceIdType.MESH

LANES = 128
SCALE = 2.0**-6

(OWN, CORE, X, YPA, YMA, YPB, YMB, YPC, YMC, YPD, YMD,
 M1P, M1M, M2AP, M2AM, M2BP, M2BM, MX, OUTC, OUTL) = range(20)
KINDS = 20


def encode(x):
    x = x * SCALE
    x3 = x * x * x
    x6 = x3 * x3
    return (x6 * x6).astype(jnp.bfloat16)


def decode(y):
    y = y.astype(jnp.float32)
    root = jnp.exp2(jnp.log(y) * (1.0 / (12.0 * 0.6931471805599453)) + 6.0)
    return jnp.where(y > 0.0, root, 0.0)


def kernel(chunks, slots, tab, keep, blocks, slab, e_out, mass_out,
           a_buf, b_buf, b_cmp, q_buf, s_buf, t_buf,
           m1s, m1r, m2as, m2ar, m2bs, m2br, mxs, mxr, fin, ms, mr, mfin,
           send, recv, a_send, a_recv, mass_send, mass_recv, cmp_sem):
    i = lax.axis_index("row")
    j = lax.axis_index("col")
    y = lax.rem(i, 4)
    yb = i - y
    q = lax.rem(j, 2)
    z = lax.rem(j // 2, 4)
    xh = j // 8
    zb = xh * 8 + q

    def row_y(d):
        return yb + lax.rem(y + d, 4)

    def col_z(d):
        return zb + 2 * lax.rem(z + d, 4)

    def flip(r):
        return lax.rem(r + 4, 8)

    xi = flip(i)
    yp, y2, ym = row_y(1), row_y(2), row_y(3)
    xyp, xy2, xym = flip(yp), flip(y2), flip(ym)
    jc = j + 1 - 2 * q
    jx = lax.rem(j + 8, 16)
    zp, z2, zm = lax.rem(z + 1, 4), lax.rem(z + 2, 4), lax.rem(z + 3, 4)

    dev_core = (i, jc)
    dev_x = (xi, j)
    dev_x2 = (i, jx)
    dev_yp, dev_ym = (yp, j), (ym, j)
    dev_zp, dev_zm = (i, col_z(1)), (i, col_z(3))
    mass_devs = [
        [(xi, j), (i, jx), (xi, jx)],
        [(row_y(d), j) for d in (1, 2, 3)],
        [(i, col_z(d)) for d in (1, 2, 3)],
    ]

    def cols(half, k):
        return pl.ds(pl.multiple_of(half * (chunks * LANES) + k * LANES, LANES), LANES)

    def remote(kind, k, src, dst, dev):
        return pltpu.make_async_remote_copy(
            src_ref=src, dst_ref=dst, send_sem=send.at[kind, k], recv_sem=recv.at[kind, k],
            device_id=dev, device_id_type=MESH)

    def arrived(kind, k, ref, dev):
        remote(kind, k, ref, ref, dev).wait_recv()

    def piece(k, r, first=0, count=4):
        return b_buf.at[k, pl.ds(r * 4 + first, count)]

    def own_copy(k):
        return pltpu.make_async_copy(slab.at[:, :, cols(q, k)], piece(k, i, q * 2, 2), recv.at[OWN, k])

    def core_copy(k):
        return remote(CORE, k, slab.at[:, :, cols(1 - q, k)], piece(k, i, q * 2, 2), dev_core)

    def piece_copy(kind, k, r, dev, first=0, count=4):
        return remote(kind, k, piece(k, r, first, count), piece(k, r, first, count), dev)

    def x_copy(k):
        return piece_copy(X, k, i, dev_x)

    def y_copies(k):
        return [piece_copy(YPA, k, i, dev_yp), piece_copy(YMA, k, i, dev_ym)]

    def yx_copies(k):
        return [piece_copy(YPB, k, xi, dev_yp), piece_copy(YMB, k, xi, dev_ym)]

    def fwd_copies(k):
        return [piece_copy(YPC, k, ym, dev_yp, 0, 2), piece_copy(YMC, k, yp, dev_ym, 2, 2)]

    def fwdx_copies(k):
        return [piece_copy(YPD, k, xym, dev_yp, 0, 2), piece_copy(YMD, k, xyp, dev_ym, 2, 2)]

    def pair_copies(kp, k, src, dst):
        slot = lax.rem(k, 2)
        return [remote(kp, k, src.at[slot, 0], dst.at[k, 0], dev_zp),
                remote(kp + 1, k, src.at[slot, 1], dst.at[k, 1], dev_zm)]

    def m1_copies(k):
        return pair_copies(M1P, k, m1s, m1r)

    def m2a_copies(k):
        return pair_copies(M2AP, k, m2as, m2ar)

    def m2b_copies(k):
        return pair_copies(M2BP, k, m2bs, m2br)

    def mx_copy(k):
        return remote(MX, k, mxs.at[lax.rem(k, 2)], mxr.at[k], dev_x2)

    def outc_copy(k):
        return remote(OUTC, k, fin.at[lax.rem(k, 2), pl.ds((1 - q) * 2, 2)], e_out.at[:, :, cols(q, k)], dev_core)

    def outl_copy(k):
        return pltpu.make_async_copy(fin.at[lax.rem(k, 2), pl.ds(q * 2, 2)], e_out.at[:, :, cols(q, k)], recv.at[OUTL, k])

    def a_local():
        return pltpu.make_async_copy(blocks, a_buf.at[pl.ds(q * slots, slots)], a_recv.at[0])

    def a_remote():
        mine = a_buf.at[pl.ds(q * slots, slots)]
        return pltpu.make_async_remote_copy(
            src_ref=blocks, dst_ref=mine, send_sem=a_send.at[0], recv_sem=a_recv.at[1],
            device_id=dev_core, device_id_type=MESH)

    def start(copies):
        for copy in copies:
            copy.start()

    barrier = pltpu.get_barrier_semaphore()
    others = [dev_core] + mass_devs[0] + mass_devs[1] + mass_devs[2]
    for dev in others:
        pl.semaphore_signal(barrier, inc=1, device_id=dev, device_id_type=MESH)
    pl.semaphore_wait(barrier, len(others))

    def stage_a(k):
        own_copy(k).wait()
        arrived(CORE, k, piece(k, i, (1 - q) * 2, 2), dev_core)
        x_copy(k).start()
        start(y_copies(k))

    def stage_b(k):
        arrived(X, k, piece(k, xi), dev_x)
        start(yx_copies(k))

    def stage_c(k):
        arrived(YPA, k, piece(k, ym), dev_ym)
        arrived(YMA, k, piece(k, yp), dev_yp)
        start(fwd_copies(k))
        arrived(YPB, k, piece(k, xym), dev_ym)
        arrived(YMB, k, piece(k, xyp), dev_yp)
        start(fwdx_copies(k))

    def partial(r):
        return q_buf[tab[4 * slots + r]]

    def compute(k):
        arrived(YPC, k, piece(k, y2, 0, 2), dev_ym)
        arrived(YMC, k, piece(k, y2, 2, 2), dev_yp)
        arrived(YPD, k, piece(k, xy2, 0, 2), dev_ym)
        arrived(YMD, k, piece(k, xy2, 2, 2), dev_yp)
        move = pltpu.make_async_copy(b_buf.at[k], b_cmp, cmp_sem.at[0])
        move.start()
        move.wait()

        def product(p, _):
            q_buf[p + 1] = keep[p] * q_buf[p] + jnp.dot(
                a_buf[tab[p]], b_cmp[tab[2 * slots + p]], preferred_element_type=jnp.float32)
            return 0

        lax.fori_loop(0, 2 * slots, product, 0)

        slot = lax.rem(k, 2)

        @pl.when(k >= 2)
        def _():
            for copy in m1_copies(k - 2) + m2a_copies(k - 2):
                copy.wait_send()

        def pack1(n, _):
            m1s[slot, 0, n] = encode(partial(z2 * 4 + n))
            m1s[slot, 1, n] = encode(partial(16 + z2 * 4 + n))
            return 0

        lax.fori_loop(0, 4, pack1, 0)
        start(m1_copies(k))

        def pack2(n, _):
            m2as[slot, 0, n] = encode(partial(16 + zp * 4 + n))
            m2as[slot, 1, n] = encode(partial(zm * 4 + n))
            return 0

        lax.fori_loop(0, 4, pack2, 0)
        start(m2a_copies(k))

        keep_slot = lax.rem(k, 3)

        def hold(n, _):
            t_buf[0, n] = partial(zp * 4 + n)
            t_buf[1, n] = partial(16 + zm * 4 + n)
            s_buf[keep_slot, 0, n] = partial(z * 4 + n)
            s_buf[keep_slot, 1, n] = partial(16 + z * 4 + n)
            return 0

        lax.fori_loop(0, 4, hold, 0)

    def relay(k):
        slot = lax.rem(k, 2)

        @pl.when(k >= 2)
        def _():
            for copy in m2b_copies(k - 2):
                copy.wait_send()

        arrived(M1P, k, m1r.at[k, 0], dev_zm)
        arrived(M1M, k, m1r.at[k, 1], dev_zp)

        def pack(n, _):
            for d in range(2):
                m2bs[slot, d, n] = encode(t_buf[d, n] + decode(m1r[k, d, n]))
            return 0

        lax.fori_loop(0, 4, pack, 0)
        start(m2b_copies(k))

    def collect(k):
        slot = lax.rem(k, 2)
        keep_slot = lax.rem(k, 3)

        @pl.when(k >= 2)
        def _():
            mx_copy(k - 2).wait_send()

        arrived(M2AP, k, m2ar.at[k, 0], dev_zm)
        arrived(M2AM, k, m2ar.at[k, 1], dev_zp)
        arrived(M2BP, k, m2br.at[k, 0], dev_zm)
        arrived(M2BM, k, m2br.at[k, 1], dev_zp)

        def total(h, n):
            return s_buf[keep_slot, h, n] + (decode(m2br[k, h, n]) + decode(m2ar[k, 1 - h, n]))

        def pack(n, _):
            mxs[slot, n] = encode(total(1 - xh, n))
            return 0

        lax.fori_loop(0, 4, pack, 0)
        mx_copy(k).start()

        def hold(n, _):
            s_buf[keep_slot, xh, n] = total(xh, n)
            return 0

        lax.fori_loop(0, 4, hold, 0)

    lane_row = lax.broadcasted_iota(jnp.int32, (8, LANES), 0)

    def finish(k):
        slot = lax.rem(k, 2)
        keep_slot = lax.rem(k, 3)

        @pl.when(k >= 2)
        def _():
            outc_copy(k - 2).wait_send()
            outl_copy(k - 2).wait()

        arrived(MX, k, mxr.at[k], dev_x2)

        def add(n, acc):
            value = s_buf[keep_slot, xh, n] + decode(mxr[k, n])
            fin[slot, n] = value
            return acc + jnp.sum((value * value).reshape(-1, 8, LANES), axis=0)

        acc = lax.fori_loop(0, 4, add, jnp.zeros((8, LANES), jnp.float32))
        outc_copy(k).start()
        outl_copy(k).start()
        ms[0] = jnp.where(lane_row == k, jnp.sum(acc, axis=0, keepdims=True), ms[0])

    def first(k, _):
        own_copy(k).start()
        core_copy(k).start()
        return 0

    lax.fori_loop(0, 2, first, 0)
    a_local().start()
    a_remote().start()
    lax.fori_loop(2, chunks, first, 0)
    q_buf[0] = jnp.zeros(q_buf.shape[1:], jnp.float32)
    ms[0] = jnp.zeros((8, LANES), jnp.float32)

    stage_a(0)
    stage_b(0)
    stage_a(1)
    a_local().wait()
    pltpu.make_async_remote_copy(
        src_ref=blocks, dst_ref=a_buf.at[pl.ds((1 - q) * slots, slots)], send_sem=a_send.at[0],
        recv_sem=a_recv.at[1], device_id=dev_core, device_id_type=MESH).wait_recv()

    def step(t, _):
        @pl.when(t < chunks)
        def _():
            stage_c(t)

        @pl.when(t + 1 < chunks)
        def _():
            stage_b(t + 1)

        @pl.when(t + 2 < chunks)
        def _():
            stage_a(t + 2)

        @pl.when((t >= 1) & (t - 1 < chunks))
        def _():
            relay(t - 1)

        @pl.when((t >= 2) & (t - 2 < chunks))
        def _():
            collect(t - 2)

        @pl.when(t >= 3)
        def _():
            finish(t - 3)

        @pl.when(t < chunks)
        def _():
            compute(t)

        return 0

    lax.fori_loop(0, chunks + 3, step, 0)

    for stage in range(3):
        copies = []
        for n, dev in enumerate(mass_devs[stage]):
            copies.append(pltpu.make_async_remote_copy(
                src_ref=ms.at[stage], dst_ref=mr.at[stage, n], send_sem=mass_send.at[stage, n],
                recv_sem=mass_recv.at[stage, n], device_id=dev, device_id_type=MESH))
        start(copies)
        for copy in copies:
            copy.wait()
        ms[stage + 1] = (ms[stage] + mr[stage, 0]) + (mr[stage, 1] + mr[stage, 2])
    last = pltpu.make_async_remote_copy(
        src_ref=ms.at[3], dst_ref=mfin, send_sem=mass_send.at[3, 0], recv_sem=mass_recv.at[3, 0],
        device_id=dev_core, device_id_type=MESH)
    last.start()
    last.wait()
    mass_out[q] = ms[3]
    mass_out[1 - q] = mfin[...]

    a_remote().wait_send()

    def drain(k, _):
        core_copy(k).wait_send()
        x_copy(k).wait_send()
        for copy in y_copies(k) + yx_copies(k) + fwd_copies(k) + fwdx_copies(k):
            copy.wait_send()
        arrived(OUTC, k, e_out.at[:, :, cols(1 - q, k)], dev_core)
        return 0

    lax.fori_loop(0, chunks, drain, 0)

    def drain_last(k, _):
        for copy in m1_copies(k) + m2a_copies(k) + m2b_copies(k):
            copy.wait_send()
        mx_copy(k).wait_send()
        outc_copy(k).wait_send()
        outl_copy(k).wait()
        return 0

    lax.fori_loop(chunks - 2, chunks, drain_last, 0)


def tables(block_rows, block_cols, live_count):
    slots = block_rows.shape[-1]
    q = lax.axis_index("col") % 2
    rows = block_rows.reshape(slots) - lax.axis_index("row") * 32
    cols = block_cols.reshape(slots)
    c = cols // 2 // 16 * 2 + cols % 2
    place = c // 2 * 4 + q * 2 + c % 2
    key = jnp.where(jnp.arange(slots) < live_count.reshape(()), rows, 32)
    mine = jnp.stack([key, place])
    other = lax.ppermute(mine, "col", [(n, n + 1 - 2 * (n % 2)) for n in range(16)])
    key = jnp.concatenate([mine[0], other[0]])
    place = jnp.concatenate([mine[1], other[1]])
    number = jnp.arange(2 * slots)
    block = jnp.where(number < slots, q * slots + number, (1 - q) * slots + number - slots)
    before = (key[:, None] < key[None, :]) | ((key[:, None] == key[None, :]) & (number[:, None] < number[None, :]))
    rank = jnp.sum(before, axis=0)
    hit = rank[None, :] == number[:, None]
    block = jnp.sum(jnp.where(hit, block[None, :], 0), axis=1)
    place = jnp.sum(jnp.where(hit, place[None, :], 0), axis=1)
    again = jnp.any((rank[None, :] + 1 == rank[:, None]) & (key[None, :] == key[:, None]), axis=1)
    keep = jnp.any(hit & again[None, :], axis=1).astype(jnp.float32)
    row = jnp.arange(32)
    upto = jnp.sum(key[None, :] <= row[:, None], axis=1)
    last = jnp.where(jnp.any(key[None, :] == row[:, None], axis=1), upto, 0)
    return jnp.concatenate([block, place, last]).astype(jnp.int32), keep


def body(blocks, block_rows, block_cols, live_count, slab):
    slots, bs = blocks.shape[2], blocks.shape[3]
    depth, width = slab.shape
    chunks = width // 2 // LANES
    tab, keep = tables(block_rows, block_cols, live_count)
    f32, bf16 = jnp.float32, jnp.bfloat16
    tile = (bs, LANES)
    vm = pltpu.VMEM
    e, mass = pl.pallas_call(
        functools.partial(kernel, chunks, slots),
        out_shape=(jax.ShapeDtypeStruct((2, bs, width), f32), jax.ShapeDtypeStruct((2, chunks, LANES), f32)),
        in_specs=[pl.BlockSpec(memory_space=pltpu.SMEM), pl.BlockSpec(memory_space=pltpu.SMEM),
                  pl.BlockSpec(memory_space=pl.ANY), pl.BlockSpec(memory_space=pl.ANY)],
        out_specs=(pl.BlockSpec(memory_space=pl.ANY), pl.BlockSpec(memory_space=pltpu.VMEM)),
        scratch_shapes=[
            vm((2 * slots, bs, bs), bf16),
            vm((chunks, 32) + tile, bf16),
            vm((32,) + tile, bf16),
            vm((2 * slots + 1,) + tile, f32),
            vm((3, 2, 4) + tile, f32),
            vm((2, 4) + tile, f32),
            vm((2, 2, 4) + tile, bf16), vm((chunks, 2, 4) + tile, bf16),
            vm((2, 2, 4) + tile, bf16), vm((chunks, 2, 4) + tile, bf16),
            vm((2, 2, 4) + tile, bf16), vm((chunks, 2, 4) + tile, bf16),
            vm((2, 4) + tile, bf16), vm((chunks, 4) + tile, bf16),
            vm((2, 4) + tile, f32),
            vm((4, chunks, LANES), f32), vm((3, 3, chunks, LANES), f32), vm((chunks, LANES), f32),
            pltpu.SemaphoreType.DMA((KINDS, chunks)), pltpu.SemaphoreType.DMA((KINDS, chunks)),
            pltpu.SemaphoreType.DMA((1,)), pltpu.SemaphoreType.DMA((2,)),
            pltpu.SemaphoreType.DMA((4, 3)), pltpu.SemaphoreType.DMA((4, 3)),
            pltpu.SemaphoreType.DMA((1,)),
        ],
        compiler_params=pltpu.CompilerParams(
            collective_id=0, has_side_effects=True, vmem_limit_bytes=58 * 1024 * 1024),
        cost_estimate=pl.CostEstimate(
            flops=2 * 2 * slots * bs * bs * width // 2, bytes_accessed=16 * 2**20, transcendentals=0),
    )(tab, keep, blocks.reshape(slots, bs, bs), slab.reshape(2, bs, width))
    expanded = e.reshape(depth, width)
    proteins = depth * 128
    return proteins * (expanded * expanded) / mass.reshape(width)


def solution(mesh):
    placed = (
        P("row", "col", None, None, None),
        P("row", "col", None),
        P("row", "col", None),
        P("row", "col"),
        P(("row", "col"), None),
    )
    return jax.shard_map(
        body, mesh=mesh, in_specs=placed, out_specs=P(("row", "col"), None), check_vma=False
    )
```

time: 896 us -> 219 us (0.24)
  waiting for transfers between devices: 625 us -> 0.01 us
  Pallas kernels: 0 us -> 208 us
  other arithmetic: 103 us -> 9.17 us
  blocking collectives: 65.9 us -> 0 us
  local copies, waits for them, and re-layouts: 52.8 us -> 0.01 us
  matrix products: 35.6 us -> 0 us
  between operations: 13.4 us -> 0.73 us
    reduce_scatter x1 -> x0, waiting for transfers between devices: 450 us -> none  [body(): lax.psum_scatter(partial_value, 'col', scatter_dimension=0, tiled=True)]
    pallas_call x0 -> x1, Pallas kernels: none -> 208 us  [body(): pl.pallas_call(functools.partial(kernel, chunks, slots), out_shape=(jax.S...]
    all_gather x1 -> x0, waiting for transfers between devices: 174 us -> none  [body(): gathered = lax.all_gather(slab, 'row', axis=0, tiled=True)]
    scatter-add x3 -> x0, other arithmetic: 92.1 us -> none  [add_group(): return partial_value.at[row_index].add(product * in_use[:, None, None])]
    psum x1 -> x0, blocking collectives: 65.9 us -> none  [body(): column_mass = lax.psum(jnp.sum(square, axis=0), ('row', 'col'))]
    dot_general x3 -> x0, matrix products: 35.6 us -> none  [add_group(): jnp.einsum('sab,sbk->sak', chosen, pieces, preferred_element_type=jnp.flo...]
    gather x3 -> x0, local copies, waits for them, and re-layouts: 31.6 us -> none  [add_group(): pieces = slab_table[col_index]]
    broadcast_in_dim x1 -> x0, local copies, waits for them, and re-layouts: 21.2 us -> none  [body(): jnp.zeros((tile_height, block_size, slab_width), jnp.float32)]
  transfers between devices with their start and end apart: 2 -> 1, of which waited for: 2 -> 0; matrix products, arithmetic and copies ran while one was open for 0% -> 1% of each run, Pallas kernels for 0% -> 0%
where the time goes in v1:
time: 219 us
  Pallas kernels  208 us (95%)
  other arithmetic  9.17 us (4%)
    pallas_call x1, Pallas kernels, body(): pl.pallas_call(functools.partial(kernel, chunks, slots), out_shape=(jax.S...  208 us
  transfers between devices with their start and end apart: 1, of which 0 were waited for; matrix products, arithmetic and copies ran while one was open for 1% of the time, Pallas kernels for 0%

profile of v1, /device:TPU:1, one launch (start us, length us, event | category | flops | bytes accessed | tf_op | source)
XLA Modules:
  0.0 219.3 jit_solution(2067150872861892751)
XLA Ops:
  0.7 0.7 compare_select_fusion.1
  1.4 1.5 collective-permute-start
  2.9 0.7 fusion.8
  3.6 0.7 compare_select_fusion.2
  4.2 0.0 collective-permute-done
  4.2 0.1 pad_add_fusion.1
  4.3 0.1 convert_reduce_fusion
  4.4 0.1 convert_reduce_fusion.1
  4.5 0.1 fusion.4
  4.7 0.2 and_reduce_fusion
  4.8 0.1 fusion.3
  5.0 0.6 convert_element_type.11.keep
  5.5 0.1 pad_add_fusion.2
  5.6 0.1 select_reduce_fusion.1
  5.7 0.6 pad_add_fusion.3.tab
  6.3 207.9 %shard_map.55 = (f32[2,256,2048]{2,1,0:T(8,128)}, f32[2,8,128]{2,1,0:T(8,128)}) custom-call(s32[128]{0:T(128)} %pad_add_fusion.3.tab, f32[48]{0:T(128)} %convert_element_type.11.keep, bf16[24,256,256]{2,1,0:T(8,128)(2,1)} %bitcast.47, bf16[2,256,2048]{2,1,0:T(8,128)(2,1)} %bitcast.48), custom_call_target="tpu_custom_call" | custom-call | flops 6442450944 | bytes 16777216 | tf_op jit(solution)/shard_map/pallas_call | solution.py:424
  214.2 0.0 copy-start
  214.2 2.6 %multiply_multiply_fusion = f32[2,256,2048]{2,1,0:T(8,128)S(1)} fusion(f32[2,256,2048]{2,1,0:T(8,128)} %get-tuple-element.7), kind=kLoop, calls=%fused_computation.1 | loop fusion | flops 2097152 | bytes 8388608 | tf_op jit(solution)/shard_map/mul | solution.py:455
  216.9 0.0 copy-done
  216.9 2.4 %bitcast_divide_fusion = f32[512,2048]{1,0:T(8,128)} fusion(f32[2,256,2048]{2,1,0:T(8,128)S(1)} %multiply_multiply_fusion, f32[2048]{0:T(1024)S(1)} %bitcast.46), kind=kLoop, calls=%fused_computation | loop fusion | flops 1048576 | bytes 8396800 | tf_op jit(solution)/shard_map/div | solution.py:455
  (5 shorter events, 0.0 us)
Async XLA Ops:
  1.4 2.9 %collective-permute-start = (s32[2,24]{1,0:T(2,128)S(1)}, s32[2,24]{1,0:T(2,128)S(1)}, u32[]{:S(2)}, u32[]{:S(2)}) collective-permute-start(s32[2,24]{1,0:T(2,128)S(1)} %pad_add_fusion), channel_id=1, source_target_pairs={{0,1},{1,0},{2,3},{3,2},{4,5},{5,4},{6,7},{7,6},{8,9},{9,8},{10,11... | collective-permute-start | bytes 584 | tf_op jit(solution)/shard_map/ppermute | solution.py:398
  214.2 2.6 %copy-start = (f32[2,8,128]{2,1,0:T(8,128)S(1)}, f32[2,8,128]{2,1,0:T(8,128)}, u32[]{:S(2)}) copy-start(f32[2,8,128]{2,1,0:T(8,128)} %get-tuple-element.8) | copy-start | bytes 24580

commit v2 on v1

--- a/solution.py
+++ b/solution.py
@@ -8,13 +8,14 @@
 from jax.sharding import PartitionSpec as P
 
 MESH = pl.DeviceIdType.MESH
+LOW, HIGH = pl.ds(0, 128), pl.ds(128, 128)
 
 LANES = 128
 SCALE = 2.0**-6
 
 (OWN, CORE, X, YPA, YMA, YPB, YMB, YPC, YMC, YPD, YMD,
- M1P, M1M, M2AP, M2AM, M2BP, M2BM, MX, OUTC, OUTL) = range(20)
-KINDS = 20
+ M1P, M1M, M2AP, M2AM, M2BP, M2BM, MX, OUTC, OUTL, X1, EAP, EAM, EBP, EBM) = range(25)
+KINDS = 25
 
 
 def encode(x):
@@ -32,7 +33,8 @@
 
 def kernel(chunks, slots, tab, keep, blocks, slab, e_out, mass_out,
            a_buf, b_buf, b_cmp, q_buf, s_buf, t_buf,
-           m1s, m1r, m2as, m2ar, m2bs, m2br, mxs, mxr, fin, ms, mr, mfin,
+           m1s, m1r, m2as, m2ar, m2bs, m2br, mxs, mxr, x1s, x1r, eas, ear, ebs, ebr, u_buf, v_buf,
+           fin, ms, mr_plane, mr_line,
            send, recv, a_send, a_recv, mass_send, mass_recv, cmp_sem):
     i = lax.axis_index("row")
     j = lax.axis_index("col")
@@ -64,11 +66,9 @@
     dev_x2 = (i, jx)
     dev_yp, dev_ym = (yp, j), (ym, j)
     dev_zp, dev_zm = (i, col_z(1)), (i, col_z(3))
-    mass_devs = [
-        [(xi, j), (i, jx), (xi, jx)],
-        [(row_y(d), j) for d in (1, 2, 3)],
-        [(i, col_z(d)) for d in (1, 2, 3)],
-    ]
+    plane = [(lax.rem(yb + 4 * fx, 8) + lax.rem(y + d, 4), lax.rem(j + 8 * fh, 16))
+             for fx in range(2) for d in range(4) for fh in range(2)][1:]
+    line = [(i, col_z(d)) for d in (1, 2, 3)] + [(i, col_z(d) + 1 - 2 * q) for d in range(4)]
 
     def cols(half, k):
         return pl.ds(pl.multiple_of(half * (chunks * LANES) + k * LANES, LANES), LANES)
@@ -121,6 +121,15 @@
 
     def m2b_copies(k):
         return pair_copies(M2BP, k, m2bs, m2br)
+
+    def x1_copy(k):
+        return remote(X1, k, x1s.at[lax.rem(k, 2)], x1r.at[k], dev_x2)
+
+    def ea_copies(k):
+        return pair_copies(EAP, k, eas, ear)
+
+    def eb_copies(k):
+        return pair_copies(EBP, k, ebs, ebr)
 
     def mx_copy(k):
         return remote(MX, k, mxs.at[lax.rem(k, 2)], mxr.at[k], dev_x2)
@@ -145,7 +154,7 @@
             copy.start()
 
     barrier = pltpu.get_barrier_semaphore()
-    others = [dev_core] + mass_devs[0] + mass_devs[1] + mass_devs[2]
+    others = plane + line
     for dev in others:
         pl.semaphore_signal(barrier, inc=1, device_id=dev, device_id_type=MESH)
     pl.semaphore_wait(barrier, len(others))
@@ -185,21 +194,29 @@
                 a_buf[tab[p]], b_cmp[tab[2 * slots + p]], preferred_element_type=jnp.float32)
             return 0
 
-        lax.fori_loop(0, 2 * slots, product, 0)
+        lax.fori_loop(0, 2 * slots, product, 0, unroll=8)
 
         slot = lax.rem(k, 2)
 
         @pl.when(k >= 2)
         def _():
+            x1_copy(k - 2).wait_send()
             for copy in m1_copies(k - 2) + m2a_copies(k - 2):
                 copy.wait_send()
+
+        def pack0(n, _):
+            x1s[slot, n] = encode(partial((1 - xh) * 16 + n * 4 + 3))
+            return 0
+
+        lax.fori_loop(0, 4, pack0, 0)
+        x1_copy(k).start()
 
         def pack1(n, _):
             m1s[slot, 0, n] = encode(partial(z2 * 4 + n))
             m1s[slot, 1, n] = encode(partial(16 + z2 * 4 + n))
             return 0
 
-        lax.fori_loop(0, 4, pack1, 0)
+        lax.fori_loop(0, 3, pack1, 0)
         start(m1_copies(k))
 
         def pack2(n, _):
@@ -207,7 +224,7 @@
             m2as[slot, 1, n] = encode(partial(zm * 4 + n))
             return 0
 
-        lax.fori_loop(0, 4, pack2, 0)
+        lax.fori_loop(0, 3, pack2, 0)
         start(m2a_copies(k))
 
         keep_slot = lax.rem(k, 3)
@@ -219,14 +236,21 @@
             s_buf[keep_slot, 1, n] = partial(16 + z * 4 + n)
             return 0
 
-        lax.fori_loop(0, 4, hold, 0)
+        lax.fori_loop(0, 3, hold, 0)
+
+        def hold_last(n, _):
+            u_buf[n] = partial(xh * 16 + n * 4 + 3)
+            return 0
+
+        lax.fori_loop(0, 4, hold_last, 0)
 
     def relay(k):
         slot = lax.rem(k, 2)
+        keep_slot = lax.rem(k, 3)
 
         @pl.when(k >= 2)
         def _():
-            for copy in m2b_copies(k - 2):
+            for copy in m2b_copies(k - 2) + ea_copies(k - 2):
                 copy.wait_send()
 
         arrived(M1P, k, m1r.at[k, 0], dev_zm)
@@ -237,8 +261,21 @@
                 m2bs[slot, d, n] = encode(t_buf[d, n] + decode(m1r[k, d, n]))
             return 0
 
-        lax.fori_loop(0, 4, pack, 0)
+        lax.fori_loop(0, 3, pack, 0)
         start(m2b_copies(k))
+
+        arrived(X1, k, x1r.at[k], dev_x2)
+
+        def join(n, _):
+            v_buf[keep_slot, n] = u_buf[n] + decode(x1r[k, n])
+            return 0
+
+        lax.fori_loop(0, 4, join, 0)
+        eas[slot, 0, 0] = encode(v_buf[keep_slot, z2, LOW])
+        eas[slot, 0, 1] = encode(v_buf[keep_slot, zp, HIGH])
+        eas[slot, 1, 0] = encode(v_buf[keep_slot, z2, HIGH])
+        eas[slot, 1, 1] = encode(v_buf[keep_slot, zm, LOW])
+        start(ea_copies(k))
 
     def collect(k):
         slot = lax.rem(k, 2)
@@ -247,6 +284,8 @@
         @pl.when(k >= 2)
         def _():
             mx_copy(k - 2).wait_send()
+            for copy in eb_copies(k - 2):
+                copy.wait_send()
 
         arrived(M2AP, k, m2ar.at[k, 0], dev_zm)
         arrived(M2AM, k, m2ar.at[k, 1], dev_zp)
@@ -260,14 +299,20 @@
             mxs[slot, n] = encode(total(1 - xh, n))
             return 0
 
-        lax.fori_loop(0, 4, pack, 0)
+        lax.fori_loop(0, 3, pack, 0)
         mx_copy(k).start()
+
+        arrived(EAP, k, ear.at[k, 0], dev_zm)
+        arrived(EAM, k, ear.at[k, 1], dev_zp)
+        ebs[slot, 0] = encode(v_buf[keep_slot, zp, LOW] + decode(ear[k, 0, 0]))
+        ebs[slot, 1] = encode(v_buf[keep_slot, zm, HIGH] + decode(ear[k, 1, 0]))
+        start(eb_copies(k))
 
         def hold(n, _):
             s_buf[keep_slot, xh, n] = total(xh, n)
             return 0
 
-        lax.fori_loop(0, 4, hold, 0)
+        lax.fori_loop(0, 3, hold, 0)
 
     lane_row = lax.broadcasted_iota(jnp.int32, (8, LANES), 0)
 
@@ -279,6 +324,14 @@
         def _():
             outc_copy(k - 2).wait_send()
             outl_copy(k - 2).wait()
+
+        arrived(EBP, k, ebr.at[k, 0], dev_zm)
+        arrived(EBM, k, ebr.at[k, 1], dev_zp)
+        low = v_buf[keep_slot, z, LOW] + (decode(ebr[k, 0]) + decode(ear[k, 1, 1]))
+        high = v_buf[keep_slot, z, HIGH] + (decode(ebr[k, 1]) + decode(ear[k, 0, 1]))
+        fin[slot, 3, LOW] = low
+        fin[slot, 3, HIGH] = high
+        acc = jnp.sum((low * low + high * high).reshape(-1, 8, LANES), axis=0)
 
         arrived(MX, k, mxr.at[k], dev_x2)
 
@@ -287,7 +340,7 @@
             fin[slot, n] = value
             return acc + jnp.sum((value * value).reshape(-1, 8, LANES), axis=0)
 
-        acc = lax.fori_loop(0, 4, add, jnp.zeros((8, LANES), jnp.float32))
+        acc = lax.fori_loop(0, 3, add, acc)
         outc_copy(k).start()
         outl_copy(k).start()
         ms[0] = jnp.where(lane_row == k, jnp.sum(acc, axis=0, keepdims=True), ms[0])
@@ -345,23 +398,21 @@
 
     lax.fori_loop(0, chunks + 3, step, 0)
 
-    for stage in range(3):
-        copies = []
-        for n, dev in enumerate(mass_devs[stage]):
-            copies.append(pltpu.make_async_remote_copy(
-                src_ref=ms.at[stage], dst_ref=mr.at[stage, n], send_sem=mass_send.at[stage, n],
-                recv_sem=mass_recv.at[stage, n], device_id=dev, device_id_type=MESH))
-        start(copies)
-        for copy in copies:
-            copy.wait()
-        ms[stage + 1] = (ms[stage] + mr[stage, 0]) + (mr[stage, 1] + mr[stage, 2])
-    last = pltpu.make_async_remote_copy(
-        src_ref=ms.at[3], dst_ref=mfin, send_sem=mass_send.at[3, 0], recv_sem=mass_recv.at[3, 0],
-        device_id=dev_core, device_id_type=MESH)
-    last.start()
-    last.wait()
-    mass_out[q] = ms[3]
-    mass_out[1 - q] = mfin[...]
+    copies = [pltpu.make_async_remote_copy(
+        src_ref=ms.at[0], dst_ref=mr_plane.at[n], send_sem=mass_send.at[n], recv_sem=mass_recv.at[n],
+        device_id=dev, device_id_type=MESH) for n, dev in enumerate(plane)]
+    start(copies)
+    for copy in copies:
+        copy.wait()
+    ms[1] = ms[0] + jnp.sum(mr_plane[...], axis=0)
+    copies = [pltpu.make_async_remote_copy(
+        src_ref=ms.at[1], dst_ref=mr_line.at[n], send_sem=mass_send.at[15 + n], recv_sem=mass_recv.at[15 + n],
+        device_id=dev, device_id_type=MESH) for n, dev in enumerate(line)]
+    start(copies)
+    for copy in copies:
+        copy.wait()
+    mass_out[q] = ms[1] + jnp.sum(mr_line[0:3], axis=0)
+    mass_out[1 - q] = jnp.sum(mr_line[3:7], axis=0)
 
     a_remote().wait_send()
 
@@ -376,8 +427,9 @@
     lax.fori_loop(0, chunks, drain, 0)
 
     def drain_last(k, _):
-        for copy in m1_copies(k) + m2a_copies(k) + m2b_copies(k):
+        for copy in m1_copies(k) + m2a_copies(k) + m2b_copies(k) + ea_copies(k) + eb_copies(k):
             copy.wait_send()
+        x1_copy(k).wait_send()
         mx_copy(k).wait_send()
         outc_copy(k).wait_send()
         outl_copy(k).wait()
@@ -419,7 +471,7 @@
     chunks = width // 2 // LANES
     tab, keep = tables(block_rows, block_cols, live_count)
     f32, bf16 = jnp.float32, jnp.bfloat16
-    tile = (bs, LANES)
+    tile, half = (bs, LANES), (bs // 2, LANES)
     vm = pltpu.VMEM
     e, mass = pl.pallas_call(
         functools.partial(kernel, chunks, slots),
@@ -432,17 +484,21 @@
             vm((chunks, 32) + tile, bf16),
             vm((32,) + tile, bf16),
             vm((2 * slots + 1,) + tile, f32),
-            vm((3, 2, 4) + tile, f32),
+            vm((3, 2, 3) + tile, f32),
+            vm((2, 3) + tile, f32),
+            vm((2, 2, 3) + tile, bf16), vm((chunks, 2, 3) + tile, bf16),
+            vm((2, 2, 3) + tile, bf16), vm((chunks, 2, 3) + tile, bf16),
+            vm((2, 2, 3) + tile, bf16), vm((chunks, 2, 3) + tile, bf16),
+            vm((2, 3) + tile, bf16), vm((chunks, 3) + tile, bf16),
+            vm((2, 4) + tile, bf16), vm((chunks, 4) + tile, bf16),
+            vm((2, 2, 2) + half, bf16), vm((chunks, 2, 2) + half, bf16),
+            vm((2, 2) + half, bf16), vm((chunks, 2) + half, bf16),
+            vm((4,) + tile, f32), vm((3, 4) + tile, f32),
             vm((2, 4) + tile, f32),
-            vm((2, 2, 4) + tile, bf16), vm((chunks, 2, 4) + tile, bf16),
-            vm((2, 2, 4) + tile, bf16), vm((chunks, 2, 4) + tile, bf16),
-            vm((2, 2, 4) + tile, bf16), vm((chunks, 2, 4) + tile, bf16),
-            vm((2, 4) + tile, bf16), vm((chunks, 4) + tile, bf16),
-            vm((2, 4) + tile, f32),
-            vm((4, chunks, LANES), f32), vm((3, 3, chunks, LANES), f32), vm((chunks, LANES), f32),
+            vm((2, chunks, LANES), f32), vm((15, chunks, LANES), f32), vm((7, chunks, LANES), f32),
             pltpu.SemaphoreType.DMA((KINDS, chunks)), pltpu.SemaphoreType.DMA((KINDS, chunks)),
             pltpu.SemaphoreType.DMA((1,)), pltpu.SemaphoreType.DMA((2,)),
-            pltpu.SemaphoreType.DMA((4, 3)), pltpu.SemaphoreType.DMA((4, 3)),
+            pltpu.SemaphoreType.DMA((22,)), pltpu.SemaphoreType.DMA((22,)),
             pltpu.SemaphoreType.DMA((1,)),
         ],
         compiler_params=pltpu.CompilerParams(
@@ -450,9 +506,8 @@
         cost_estimate=pl.CostEstimate(
             flops=2 * 2 * slots * bs * bs * width // 2, bytes_accessed=16 * 2**20, transcendentals=0),
     )(tab, keep, blocks.reshape(slots, bs, bs), slab.reshape(2, bs, width))
-    expanded = e.reshape(depth, width)
-    proteins = depth * 128
-    return proteins * (expanded * expanded) / mass.reshape(width)
+    scale = depth * 128 / mass.reshape(1, 1, width)
+    return (e * e * scale).reshape(depth, width)
 
 
 def solution(mesh):

time: 219 us -> 202 us (0.922)
  Pallas kernels: 208 us -> 190 us
    pallas_call x1, Pallas kernels: 208 us -> 190 us  [body(): pl.pallas_call(functools.partial(kernel, chunks, slots), out_shape=(jax.S...]
    mul x1, other arithmetic: 2.63 us -> 4.97 us  [body(): return (e * e * scale).reshape(depth, width)]
where the time goes in v2:
time: 202 us
  Pallas kernels  190 us (94%)
  other arithmetic  9.77 us (5%)
    pallas_call x1, Pallas kernels, body(): pl.pallas_call(functools.partial(kernel, chunks, slots), out_shape=(jax.S...  190 us
    mul x1, other arithmetic, body(): return (e * e * scale).reshape(depth, width)  4.97 us
  transfers between devices with their start and end apart: 1, of which 0 were waited for; matrix products, arithmetic and copies ran while one was open for 1% of the time, Pallas kernels for 0%

profile of v2, /device:TPU:1, one launch (start us, length us, event | category | flops | bytes accessed | tf_op | source)
XLA Modules:
  0.0 201.9 jit_solution(1326739244511984996)
XLA Ops:
  0.7 0.7 compare_select_fusion.1
  1.4 1.5 collective-permute-start
  2.9 0.7 fusion.8
  3.6 0.7 compare_select_fusion.2
  4.2 0.0 collective-permute-done
  4.2 0.1 pad_add_fusion.1
  4.3 0.1 convert_reduce_fusion
  4.4 0.1 convert_reduce_fusion.1
  4.5 0.1 fusion.4
  4.7 0.2 and_reduce_fusion
  4.8 0.1 fusion.3
  5.0 0.6 convert_element_type.11.keep
  5.5 0.1 pad_add_fusion.2
  5.6 0.1 select_reduce_fusion.1
  5.7 0.6 pad_add_fusion.3.tab
  6.3 189.9 %shard_map.55 = (f32[2,256,2048]{2,1,0:T(8,128)}, f32[2,8,128]{2,1,0:T(8,128)}) custom-call(s32[128]{0:T(128)} %pad_add_fusion.3.tab, f32[48]{0:T(128)} %convert_element_type.11.keep, bf16[24,256,256]{2,1,0:T(8,128)(2,1)} %bitcast.46, bf16[2,256,2048]{2,1,0:T(8,128)(2,1)} %bitcast.47), custom_call_target="tpu_custom_call" | custom-call | flops 6442450944 | bytes 16777216 | tf_op jit(solution)/shard_map/pallas_call | solution.py:476
  196.2 0.7 divide_bitcast_fusion
  196.9 5.0 %multiply_multiply_fusion = f32[2,256,2048]{2,1,0:T(8,128)} fusion(f32[2,256,2048]{2,1,0:T(8,128)} %get-tuple-element.7, f32[2048]{0:T(1024)S(1)} %divide_bitcast_fusion), kind=kLoop, calls=%fused_computation | loop fusion | flops 2097152 | bytes 8396800 | tf_op jit(solution)/shard_map/mul | solution.py:510
  (5 shorter events, 0.0 us)
Async XLA Ops:
  1.4 2.9 %collective-permute-start = (s32[2,24]{1,0:T(2,128)S(1)}, s32[2,24]{1,0:T(2,128)S(1)}, u32[]{:S(2)}, u32[]{:S(2)}) collective-permute-start(s32[2,24]{1,0:T(2,128)S(1)} %pad_add_fusion), channel_id=1, source_target_pairs={{0,1},{1,0},{2,3},{3,2},{4,5},{5,4},{6,7},{7,6},{8,9},{9,8},{10,11... | collective-permute-start | bytes 584 | tf_op jit(solution)/shard_map/ppermute | solution.py:450

commit v3 on v2

--- a/solution.py
+++ b/solution.py
@@ -11,31 +11,33 @@
 LOW, HIGH = pl.ds(0, 128), pl.ds(128, 128)
 
 LANES = 128
-SCALE = 2.0**-6
-
-(OWN, CORE, X, YPA, YMA, YPB, YMB, YPC, YMC, YPD, YMD,
- M1P, M1M, M2AP, M2AM, M2BP, M2BM, MX, OUTC, OUTL, X1, EAP, EAM, EBP, EBM) = range(25)
-KINDS = 25
+FORKED = 4
+MID, POWER, FLOOR = 6.0, 26.0, 117.0
+LN2 = 0.6931471805599453
+
+(OWN, CORE, OUTC, OUTL,
+ X, YPA, YMA, YPB, YMB, YPC, YMC, YPD, YMD, XF0, XF1,
+ M1P, M1M, M2AP, M2AM, M2BP, M2BM, MX, X1, EAP, EAM, EBP, EBM) = range(27)
+WIDE, KINDS, TURNS = 4, 27, 4
 
 
 def encode(x):
-    x = x * SCALE
-    x3 = x * x * x
-    x6 = x3 * x3
-    return (x6 * x6).astype(jnp.bfloat16)
+    u = jnp.log(x) * (1.0 / LN2) - MID
+    y = jnp.exp2(jnp.abs(u) * POWER - FLOOR)
+    return jnp.where(x > 0.0, jnp.where(u < 0.0, -y, y), 0.0).astype(jnp.bfloat16)
 
 
 def decode(y):
     y = y.astype(jnp.float32)
-    root = jnp.exp2(jnp.log(y) * (1.0 / (12.0 * 0.6931471805599453)) + 6.0)
-    return jnp.where(y > 0.0, root, 0.0)
+    u = jnp.log(jnp.abs(y)) * (1.0 / (POWER * LN2)) + FLOOR / POWER
+    return jnp.where(y != 0.0, jnp.exp2(jnp.where(y < 0.0, -u, u) + MID), 0.0)
 
 
 def kernel(chunks, slots, tab, keep, blocks, slab, e_out, mass_out,
            a_buf, b_buf, b_cmp, q_buf, s_buf, t_buf,
            m1s, m1r, m2as, m2ar, m2bs, m2br, mxs, mxr, x1s, x1r, eas, ear, ebs, ebr, u_buf, v_buf,
            fin, ms, mr_plane, mr_line,
-           send, recv, a_send, a_recv, mass_send, mass_recv, cmp_sem):
+           wide_send, wide_recv, send, recv, a_send, a_recv, mass_send, mass_recv, cmp_sem):
     i = lax.axis_index("row")
     j = lax.axis_index("col")
     y = lax.rem(i, 4)
@@ -74,9 +76,12 @@
         return pl.ds(pl.multiple_of(half * (chunks * LANES) + k * LANES, LANES), LANES)
 
     def remote(kind, k, src, dst, dev):
+        if kind < WIDE:
+            sems = wide_send.at[kind, k], wide_recv.at[kind, k]
+        else:
+            sems = send.at[kind - WIDE, lax.rem(k, TURNS)], recv.at[kind - WIDE, lax.rem(k, TURNS)]
         return pltpu.make_async_remote_copy(
-            src_ref=src, dst_ref=dst, send_sem=send.at[kind, k], recv_sem=recv.at[kind, k],
-            device_id=dev, device_id_type=MESH)
+            src_ref=src, dst_ref=dst, send_sem=sems[0], recv_sem=sems[1], device_id=dev, device_id_type=MESH)
 
     def arrived(kind, k, ref, dev):
         remote(kind, k, ref, ref, dev).wait_recv()
@@ -85,7 +90,7 @@
         return b_buf.at[k, pl.ds(r * 4 + first, count)]
 
     def own_copy(k):
-        return pltpu.make_async_copy(slab.at[:, :, cols(q, k)], piece(k, i, q * 2, 2), recv.at[OWN, k])
+        return pltpu.make_async_copy(slab.at[:, :, cols(q, k)], piece(k, i, q * 2, 2), wide_recv.at[OWN, k])
 
     def core_copy(k):
         return remote(CORE, k, slab.at[:, :, cols(1 - q, k)], piece(k, i, q * 2, 2), dev_core)
@@ -99,8 +104,22 @@
     def y_copies(k):
         return [piece_copy(YPA, k, i, dev_yp), piece_copy(YMA, k, i, dev_ym)]
 
-    def yx_copies(k):
+    def yx_copies(k, forked):
+        if forked:
+            return [piece_copy(YPB, k, xi, dev_yp, 0, 3), piece_copy(YMB, k, xi, dev_ym, 1, 3)]
         return [piece_copy(YPB, k, xi, dev_yp), piece_copy(YMB, k, xi, dev_ym)]
+
+    def fork_copies(k):
+        return [piece_copy(XF0, k, ym, dev_x, 3, 1), piece_copy(XF1, k, yp, dev_x, 0, 1)]
+
+    def by_fork(k, act):
+        @pl.when(k < FORKED)
+        def _():
+            act(True)
+
+        @pl.when(k >= FORKED)
+        def _():
+            act(False)
 
     def fwd_copies(k):
         return [piece_copy(YPC, k, ym, dev_yp, 0, 2), piece_copy(YMC, k, yp, dev_ym, 2, 2)]
@@ -138,7 +157,7 @@
         return remote(OUTC, k, fin.at[lax.rem(k, 2), pl.ds((1 - q) * 2, 2)], e_out.at[:, :, cols(q, k)], dev_core)
 
     def outl_copy(k):
-        return pltpu.make_async_copy(fin.at[lax.rem(k, 2), pl.ds(q * 2, 2)], e_out.at[:, :, cols(q, k)], recv.at[OUTL, k])
+        return pltpu.make_async_copy(fin.at[lax.rem(k, 2), pl.ds(q * 2, 2)], e_out.at[:, :, cols(q, k)], wide_recv.at[OUTL, k])
 
     def a_local():
         return pltpu.make_async_copy(blocks, a_buf.at[pl.ds(q * slots, slots)], a_recv.at[0])
@@ -153,28 +172,68 @@
         for copy in copies:
             copy.start()
 
+    def sent(copies):
+        for copy in copies:
+            copy.wait_send()
+
+    def first(k, _):
+        core_copy(k).start()
+        return 0
+
+    def first_local(k, _):
+        own_copy(k).start()
+        return 0
+
+    lax.fori_loop(0, chunks, first_local, 0)
     barrier = pltpu.get_barrier_semaphore()
     others = plane + line
     for dev in others:
         pl.semaphore_signal(barrier, inc=1, device_id=dev, device_id_type=MESH)
+    a_local().start()
+    q_buf[0] = jnp.zeros(q_buf.shape[1:], jnp.float32)
+    ms[0] = jnp.zeros((8, LANES), jnp.float32)
     pl.semaphore_wait(barrier, len(others))
 
     def stage_a(k):
+        @pl.when(k >= TURNS)
+        def _():
+            sent([x_copy(k - TURNS)] + y_copies(k - TURNS))
+
         own_copy(k).wait()
         arrived(CORE, k, piece(k, i, (1 - q) * 2, 2), dev_core)
+        start(y_copies(k))
         x_copy(k).start()
-        start(y_copies(k))
 
     def stage_b(k):
+        @pl.when(k >= TURNS)
+        def _():
+            by_fork(k - TURNS, lambda forked: sent(yx_copies(k - TURNS, forked)))
+
         arrived(X, k, piece(k, xi), dev_x)
-        start(yx_copies(k))
+        by_fork(k, lambda forked: start(yx_copies(k, forked)))
 
     def stage_c(k):
+        @pl.when(k >= TURNS)
+        def _():
+            sent(fwd_copies(k - TURNS) + fwdx_copies(k - TURNS))
+
+            @pl.when(k - TURNS < FORKED)
+            def _():
+                sent(fork_copies(k - TURNS))
+
         arrived(YPA, k, piece(k, ym), dev_ym)
         arrived(YMA, k, piece(k, yp), dev_yp)
         start(fwd_copies(k))
-        arrived(YPB, k, piece(k, xym), dev_ym)
-        arrived(YMB, k, piece(k, xyp), dev_yp)
+
+        @pl.when(k < FORKED)
+        def _():
+            start(fork_copies(k))
+
+        def rest(forked):
+            arrived(YPB, k, piece(k, xym, 0, 3 if forked else 4), dev_ym)
+            arrived(YMB, k, piece(k, xyp, *((1, 3) if forked else (0, 4))), dev_yp)
+
+        by_fork(k, rest)
         start(fwdx_copies(k))
 
     def partial(r):
@@ -185,8 +244,22 @@
         arrived(YMC, k, piece(k, y2, 2, 2), dev_yp)
         arrived(YPD, k, piece(k, xy2, 0, 2), dev_ym)
         arrived(YMD, k, piece(k, xy2, 2, 2), dev_yp)
+
+        @pl.when(k < FORKED)
+        def _():
+            arrived(XF0, k, piece(k, xym, 3, 1), dev_x)
+            arrived(XF1, k, piece(k, xyp, 0, 1), dev_x)
+
         move = pltpu.make_async_copy(b_buf.at[k], b_cmp, cmp_sem.at[0])
         move.start()
+
+        @pl.when(k == 0)
+        def _():
+            a_local().wait()
+            pltpu.make_async_remote_copy(
+                src_ref=blocks, dst_ref=a_buf.at[pl.ds((1 - q) * slots, slots)], send_sem=a_send.at[0],
+                recv_sem=a_recv.at[1], device_id=dev_core, device_id_type=MESH).wait_recv()
+
         move.wait()
 
         def product(p, _):
@@ -345,25 +418,13 @@
         outl_copy(k).start()
         ms[0] = jnp.where(lane_row == k, jnp.sum(acc, axis=0, keepdims=True), ms[0])
 
-    def first(k, _):
-        own_copy(k).start()
-        core_copy(k).start()
-        return 0
-
-    lax.fori_loop(0, 2, first, 0)
-    a_local().start()
+    core_copy(0).start()
+    core_copy(1).start()
     a_remote().start()
     lax.fori_loop(2, chunks, first, 0)
-    q_buf[0] = jnp.zeros(q_buf.shape[1:], jnp.float32)
-    ms[0] = jnp.zeros((8, LANES), jnp.float32)
-
     stage_a(0)
     stage_b(0)
     stage_a(1)
-    a_local().wait()
-    pltpu.make_async_remote_copy(
-        src_ref=blocks, dst_ref=a_buf.at[pl.ds((1 - q) * slots, slots)], send_sem=a_send.at[0],
-        recv_sem=a_recv.at[1], device_id=dev_core, device_id_type=MESH).wait_recv()
 
     def step(t, _):
         @pl.when(t < chunks)
@@ -418,13 +479,17 @@
 
     def drain(k, _):
         core_copy(k).wait_send()
-        x_copy(k).wait_send()
-        for copy in y_copies(k) + yx_copies(k) + fwd_copies(k) + fwdx_copies(k):
-            copy.wait_send()
         arrived(OUTC, k, e_out.at[:, :, cols(1 - q, k)], dev_core)
         return 0
 
     lax.fori_loop(0, chunks, drain, 0)
+
+    def drain_pieces(k, _):
+        sent([x_copy(k)] + y_copies(k) + fwd_copies(k) + fwdx_copies(k))
+        by_fork(k, lambda forked: sent(yx_copies(k, forked) + (fork_copies(k) if forked else [])))
+        return 0
+
+    lax.fori_loop(chunks - TURNS, chunks, drain_pieces, 0)
 
     def drain_last(k, _):
         for copy in m1_copies(k) + m2a_copies(k) + m2b_copies(k) + ea_copies(k) + eb_copies(k):
@@ -496,7 +561,8 @@
             vm((4,) + tile, f32), vm((3, 4) + tile, f32),
             vm((2, 4) + tile, f32),
             vm((2, chunks, LANES), f32), vm((15, chunks, LANES), f32), vm((7, chunks, LANES), f32),
-            pltpu.SemaphoreType.DMA((KINDS, chunks)), pltpu.SemaphoreType.DMA((KINDS, chunks)),
+            pltpu.SemaphoreType.DMA((WIDE, chunks)), pltpu.SemaphoreType.DMA((WIDE, chunks)),
+            pltpu.SemaphoreType.DMA((KINDS - WIDE, TURNS)), pltpu.SemaphoreType.DMA((KINDS - WIDE, TURNS)),
             pltpu.SemaphoreType.DMA((1,)), pltpu.SemaphoreType.DMA((2,)),
             pltpu.SemaphoreType.DMA((22,)), pltpu.SemaphoreType.DMA((22,)),
             pltpu.SemaphoreType.DMA((1,)),

time: 202 us -> 196 us (0.970)
  Pallas kernels: 190 us -> 184 us
    pallas_call x1, Pallas kernels: 190 us -> 184 us  [body(): pl.pallas_call(functools.partial(kernel, chunks, slots), out_shape=(jax.S...]
where the time goes in v3:
time: 196 us
  Pallas kernels  184 us (94%)
  other arithmetic  9.77 us (5%)
    pallas_call x1, Pallas kernels, body(): pl.pallas_call(functools.partial(kernel, chunks, slots), out_shape=(jax.S...  184 us
    mul x1, other arithmetic, body(): return (e * e * scale).reshape(depth, width)  4.97 us
  transfers between devices with their start and end apart: 1, of which 0 were waited for; matrix products, arithmetic and copies ran while one was open for 1% of the time, Pallas kernels for 0%

profile of v3, /device:TPU:1, one launch (start us, length us, event | category | flops | bytes accessed | tf_op | source)
XLA Modules:
  0.0 195.8 jit_solution(16706721732512130651)
XLA Ops:
  0.7 0.7 compare_select_fusion.1
  1.4 1.5 collective-permute-start
  2.9 0.7 fusion.8
  3.6 0.7 compare_select_fusion.2
  4.2 0.0 collective-permute-done
  4.2 0.1 pad_add_fusion.1
  4.3 0.1 convert_reduce_fusion
  4.4 0.1 convert_reduce_fusion.1
  4.5 0.1 fusion.4
  4.7 0.2 and_reduce_fusion
  4.8 0.1 fusion.3
  5.0 0.6 convert_element_type.11.keep
  5.5 0.1 pad_add_fusion.2
  5.6 0.1 select_reduce_fusion.1
  5.7 0.6 pad_add_fusion.3.tab
  6.3 183.8 %shard_map.55 = (f32[2,256,2048]{2,1,0:T(8,128)}, f32[2,8,128]{2,1,0:T(8,128)}) custom-call(s32[128]{0:T(128)} %pad_add_fusion.3.tab, f32[48]{0:T(128)} %convert_element_type.11.keep, bf16[24,256,256]{2,1,0:T(8,128)(2,1)} %bitcast.46, bf16[2,256,2048]{2,1,0:T(8,128)(2,1)} %bitcast.47), custom_call_target="tpu_custom_call" | custom-call | flops 6442450944 | bytes 16777216 | tf_op jit(solution)/shard_map/pallas_call | solution.py:541
  190.2 0.7 divide_bitcast_fusion
  190.9 5.0 %multiply_multiply_fusion = f32[2,256,2048]{2,1,0:T(8,128)} fusion(f32[2,256,2048]{2,1,0:T(8,128)} %get-tuple-element.7, f32[2048]{0:T(1024)S(1)} %divide_bitcast_fusion), kind=kLoop, calls=%fused_computation | loop fusion | flops 2097152 | bytes 8396800 | tf_op jit(solution)/shard_map/mul | solution.py:576
  (5 shorter events, 0.0 us)
Async XLA Ops:
  1.4 2.9 %collective-permute-start = (s32[2,24]{1,0:T(2,128)S(1)}, s32[2,24]{1,0:T(2,128)S(1)}, u32[]{:S(2)}, u32[]{:S(2)}) collective-permute-start(s32[2,24]{1,0:T(2,128)S(1)} %pad_add_fusion), channel_id=1, source_target_pairs={{0,1},{1,0},{2,3},{3,2},{4,5},{5,4},{6,7},{7,6},{8,9},{9,8},{10,11... | collective-permute-start | bytes 584 | tf_op jit(solution)/shard_map/ppermute | solution.py:515

commit v4 on v3

--- a/solution.py
+++ b/solution.py
@@ -33,11 +33,12 @@
     return jnp.where(y != 0.0, jnp.exp2(jnp.where(y < 0.0, -u, u) + MID), 0.0)
 
 
-def kernel(chunks, slots, tab, keep, blocks, slab, e_out, mass_out,
+def kernel(chunks, slots, rows, columns, live, blocks, slab, e_out, mass_out,
            a_buf, b_buf, b_cmp, q_buf, s_buf, t_buf,
            m1s, m1r, m2as, m2ar, m2bs, m2br, mxs, mxr, x1s, x1r, eas, ear, ebs, ebr, u_buf, v_buf,
            fin, ms, mr_plane, mr_line,
-           wide_send, wide_recv, send, recv, a_send, a_recv, mass_send, mass_recv, cmp_sem):
+           meta, meta_in, tab_v, keep_v, tab, keep,
+           wide_send, wide_recv, send, recv, a_send, a_recv, mass_send, mass_recv, cmp_sem, meta_sems, tab_sems):
     i = lax.axis_index("row")
     j = lax.axis_index("col")
     y = lax.rem(i, 4)
@@ -184,6 +185,61 @@
         own_copy(k).start()
         return 0
 
+    def meta_copy():
+        return pltpu.make_async_remote_copy(
+            src_ref=meta, dst_ref=meta_in, send_sem=meta_sems.at[0], recv_sem=meta_sems.at[1],
+            device_id=dev_core, device_id_type=MESH)
+
+    lane = lax.broadcasted_iota(jnp.int32, (8, LANES), 1)
+
+    def list_slots():
+        number = lax.broadcasted_iota(jnp.int32, (1, slots), 1)
+        key = jnp.where(number < live[0, 0], rows[...] - i * 32, 32)
+        place = lax.shift_right_logical(columns[...], 5) * 4 + q * 2 + (columns[...] & 1)
+        meta[...] = jnp.full((8, LANES), 64, jnp.int32)
+
+        @pl.when(q == 0)
+        def _():
+            meta[0:1, 0:slots] = key
+            meta[1:2, 0:slots] = place
+
+        @pl.when(q == 1)
+        def _():
+            meta[0:1, slots:2 * slots] = key
+            meta[1:2, slots:2 * slots] = place
+
+    def make_tables():
+        meta_copy().wait()
+        joint = jnp.where((lane >= q * slots) & (lane < (q + 1) * slots), meta[...], meta_in[...])
+        square = (LANES, LANES)
+        item = lax.broadcasted_iota(jnp.int32, square, 0)
+        at = lax.broadcasted_iota(jnp.int32, square, 1)
+        key_b = jnp.broadcast_to(joint[0:1], square)
+        key_a = key_b.T
+        place_a = jnp.broadcast_to(joint[1:2], square).T
+
+        def count(mask):
+            return jnp.sum(jnp.where(mask, 1, 0), axis=0, keepdims=True)
+
+        def pick(mask, value):
+            return jnp.sum(jnp.where(mask, value, 0), axis=0, keepdims=True)
+
+        rank = count((key_a < key_b) | ((key_a == key_b) & (item < at)))
+        rank_a = jnp.broadcast_to(rank, square).T
+        hit = rank_a == at
+        key_here = pick(hit, key_a)
+        key_before = pick(rank_a + 1 == at, key_a)
+        tab_v[...] = jnp.zeros((8, LANES), jnp.int32)
+        tab_v[0:1] = pick(hit, item)
+        tab_v[1:2] = pick(hit, place_a)
+        tab_v[2:3] = jnp.where(count(key_a == at) > 0, count(key_a <= at), 0)
+        keep_v[...] = jnp.broadcast_to(
+            jnp.where((key_here == key_before) & (lane[0:1] > 0), 1.0, 0.0), (8, LANES))
+        moves = [pltpu.make_async_copy(tab_v, tab, tab_sems.at[0]), pltpu.make_async_copy(keep_v, keep, tab_sems.at[1])]
+        start(moves)
+        for move in moves:
+            move.wait()
+
     lax.fori_loop(0, chunks, first_local, 0)
     barrier = pltpu.get_barrier_semaphore()
     others = plane + line
@@ -192,7 +248,9 @@
     a_local().start()
     q_buf[0] = jnp.zeros(q_buf.shape[1:], jnp.float32)
     ms[0] = jnp.zeros((8, LANES), jnp.float32)
+    list_slots()
     pl.semaphore_wait(barrier, len(others))
+    meta_copy().start()
 
     def stage_a(k):
         @pl.when(k >= TURNS)
@@ -237,7 +295,7 @@
         start(fwdx_copies(k))
 
     def partial(r):
-        return q_buf[tab[4 * slots + r]]
+        return q_buf[tab[2, r]]
 
     def compute(k):
         arrived(YPC, k, piece(k, y2, 0, 2), dev_ym)
@@ -263,8 +321,8 @@
         move.wait()
 
         def product(p, _):
-            q_buf[p + 1] = keep[p] * q_buf[p] + jnp.dot(
-                a_buf[tab[p]], b_cmp[tab[2 * slots + p]], preferred_element_type=jnp.float32)
+            q_buf[p + 1] = keep[0, p] * q_buf[p] + jnp.dot(
+                a_buf[tab[0, p]], b_cmp[tab[1, p]], preferred_element_type=jnp.float32)
             return 0
 
         lax.fori_loop(0, 2 * slots, product, 0, unroll=8)
@@ -298,6 +356,11 @@
             return 0
 
         lax.fori_loop(0, 3, pack2, 0)
+
+        @pl.when(k == chunks - 1)
+        def _():
+            sent(m1_copies(k))
+
         start(m2a_copies(k))
 
         keep_slot = lax.rem(k, 3)
@@ -425,6 +488,7 @@
     stage_a(0)
     stage_b(0)
     stage_a(1)
+    make_tables()
 
     def step(t, _):
         @pl.when(t < chunks)
@@ -491,8 +555,10 @@
 
     lax.fori_loop(chunks - TURNS, chunks, drain_pieces, 0)
 
+    sent(m1_copies(chunks - 2))
+
     def drain_last(k, _):
-        for copy in m1_copies(k) + m2a_copies(k) + m2b_copies(k) + ea_copies(k) + eb_copies(k):
+        for copy in m2a_copies(k) + m2b_copies(k) + ea_copies(k) + eb_copies(k):
             copy.wait_send()
         x1_copy(k).wait_send()
         mx_copy(k).wait_send()
@@ -503,45 +569,18 @@
     lax.fori_loop(chunks - 2, chunks, drain_last, 0)
 
 
-def tables(block_rows, block_cols, live_count):
-    slots = block_rows.shape[-1]
-    q = lax.axis_index("col") % 2
-    rows = block_rows.reshape(slots) - lax.axis_index("row") * 32
-    cols = block_cols.reshape(slots)
-    c = cols // 2 // 16 * 2 + cols % 2
-    place = c // 2 * 4 + q * 2 + c % 2
-    key = jnp.where(jnp.arange(slots) < live_count.reshape(()), rows, 32)
-    mine = jnp.stack([key, place])
-    other = lax.ppermute(mine, "col", [(n, n + 1 - 2 * (n % 2)) for n in range(16)])
-    key = jnp.concatenate([mine[0], other[0]])
-    place = jnp.concatenate([mine[1], other[1]])
-    number = jnp.arange(2 * slots)
-    block = jnp.where(number < slots, q * slots + number, (1 - q) * slots + number - slots)
-    before = (key[:, None] < key[None, :]) | ((key[:, None] == key[None, :]) & (number[:, None] < number[None, :]))
-    rank = jnp.sum(before, axis=0)
-    hit = rank[None, :] == number[:, None]
-    block = jnp.sum(jnp.where(hit, block[None, :], 0), axis=1)
-    place = jnp.sum(jnp.where(hit, place[None, :], 0), axis=1)
-    again = jnp.any((rank[None, :] + 1 == rank[:, None]) & (key[None, :] == key[:, None]), axis=1)
-    keep = jnp.any(hit & again[None, :], axis=1).astype(jnp.float32)
-    row = jnp.arange(32)
-    upto = jnp.sum(key[None, :] <= row[:, None], axis=1)
-    last = jnp.where(jnp.any(key[None, :] == row[:, None], axis=1), upto, 0)
-    return jnp.concatenate([block, place, last]).astype(jnp.int32), keep
-
-
 def body(blocks, block_rows, block_cols, live_count, slab):
     slots, bs = blocks.shape[2], blocks.shape[3]
     depth, width = slab.shape
     chunks = width // 2 // LANES
-    tab, keep = tables(block_rows, block_cols, live_count)
     f32, bf16 = jnp.float32, jnp.bfloat16
     tile, half = (bs, LANES), (bs // 2, LANES)
     vm = pltpu.VMEM
     e, mass = pl.pallas_call(
         functools.partial(kernel, chunks, slots),
         out_shape=(jax.ShapeDtypeStruct((2, bs, width), f32), jax.ShapeDtypeStruct((2, chunks, LANES), f32)),
-        in_specs=[pl.BlockSpec(memory_space=pltpu.SMEM), pl.BlockSpec(memory_space=pltpu.SMEM),
+        in_specs=[pl.BlockSpec(memory_space=pltpu.VMEM), pl.BlockSpec(memory_space=pltpu.VMEM),
+                  pl.BlockSpec(memory_space=pltpu.SMEM),
                   pl.BlockSpec(memory_space=pl.ANY), pl.BlockSpec(memory_space=pl.ANY)],
         out_specs=(pl.BlockSpec(memory_space=pl.ANY), pl.BlockSpec(memory_space=pltpu.VMEM)),
         scratch_shapes=[
@@ -561,17 +600,19 @@
             vm((4,) + tile, f32), vm((3, 4) + tile, f32),
             vm((2, 4) + tile, f32),
             vm((2, chunks, LANES), f32), vm((15, chunks, LANES), f32), vm((7, chunks, LANES), f32),
+            vm((8, LANES), jnp.int32), vm((8, LANES), jnp.int32), vm((8, LANES), jnp.int32), vm((8, LANES), f32),
+            pltpu.SMEM((8, LANES), jnp.int32), pltpu.SMEM((8, LANES), f32),
             pltpu.SemaphoreType.DMA((WIDE, chunks)), pltpu.SemaphoreType.DMA((WIDE, chunks)),
             pltpu.SemaphoreType.DMA((KINDS - WIDE, TURNS)), pltpu.SemaphoreType.DMA((KINDS - WIDE, TURNS)),
             pltpu.SemaphoreType.DMA((1,)), pltpu.SemaphoreType.DMA((2,)),
             pltpu.SemaphoreType.DMA((22,)), pltpu.SemaphoreType.DMA((22,)),
-            pltpu.SemaphoreType.DMA((1,)),
+            pltpu.SemaphoreType.DMA((1,)), pltpu.SemaphoreType.DMA((2,)), pltpu.SemaphoreType.DMA((2,)),
         ],
         compiler_params=pltpu.CompilerParams(
             collective_id=0, has_side_effects=True, vmem_limit_bytes=58 * 1024 * 1024),
         cost_estimate=pl.CostEstimate(
             flops=2 * 2 * slots * bs * bs * width // 2, bytes_accessed=16 * 2**20, transcendentals=0),
-    )(tab, keep, blocks.reshape(slots, bs, bs), slab.reshape(2, bs, width))
+    )(block_rows.reshape(1, slots), block_cols.reshape(1, slots), live_count, blocks.reshape(slots, bs, bs), slab.reshape(2, bs, width))
     scale = depth * 128 / mass.reshape(1, 1, width)
     return (e * e * scale).reshape(depth, width)
 

time: 196 us -> 192 us (0.980)
  other arithmetic: 9.77 us -> 5.67 us
  transfers between devices with their start and end apart: 1 -> 0, of which waited for: 0 -> 0; matrix products, arithmetic and copies ran while one was open for 1% -> 0% of each run, Pallas kernels for 0% -> 0%
where the time goes in v4:
time: 192 us
  Pallas kernels  185 us (96%)
  other arithmetic  5.67 us (3%)
    pallas_call x1, Pallas kernels, body(): pl.pallas_call(functools.partial(kernel, chunks, slots), out_shape=(jax.S...  185 us
    mul x1, other arithmetic, body(): return (e * e * scale).reshape(depth, width)  4.97 us

profile of v4, /device:TPU:1, one launch (start us, length us, event | category | flops | bytes accessed | tf_op | source)
XLA Modules:
  0.0 191.5 jit_solution(14812461998606889377)
XLA Ops:
  0.7 185.2 %shard_map.55 = (f32[2,256,2048]{2,1,0:T(8,128)}, f32[2,8,128]{2,1,0:T(8,128)}) custom-call(s32[1,24]{1,0:T(1,128)} %bitcast.9, s32[1,24]{1,0:T(1,128)} %bitcast.10, s32[1,1]{1,0:T(1,128)S(6)} %copy.6.live, bf16[24,256,256]{2,1,0:T(8,128)(2,1)} %bitcast.7, bf16[2,256,2048]{2,1,0:T(8,128)(2,1)} %bitcast.8), custom_call_target="tpu_custom_call" | custom-call | flops 6442450944 | bytes 16777216 | tf_op jit(solution)/shard_map/pallas_call | solution.py:579
  185.9 0.7 divide_bitcast_fusion
  186.6 5.0 %multiply_multiply_fusion = f32[2,256,2048]{2,1,0:T(8,128)} fusion(f32[2,256,2048]{2,1,0:T(8,128)} %get-tuple-element.7, f32[2048]{0:T(1024)S(1)} %divide_bitcast_fusion), kind=kLoop, calls=%fused_computation | loop fusion | flops 2097152 | bytes 8396800 | tf_op jit(solution)/shard_map/mul | solution.py:617

commit v5 on v4

--- a/solution.py
+++ b/solution.py
@@ -17,8 +17,9 @@
 
 (OWN, CORE, OUTC, OUTL,
  X, YPA, YMA, YPB, YMB, YPC, YMC, YPD, YMD, XF0, XF1,
- M1P, M1M, M2AP, M2AM, M2BP, M2BM, MX, X1, EAP, EAM, EBP, EBM) = range(27)
-WIDE, KINDS, TURNS = 4, 27, 4
+ M1P, M1M, M2AP, M2AM, X1, EAP, EAM, EBP, EBM, M2BP, M2BM, MX) = range(27)
+SPLIT = 3
+WIDE, KINDS, TURNS = 4, 27 + 3 * (SPLIT - 1), 3
 
 
 def encode(x):
@@ -30,7 +31,7 @@
 def decode(y):
     y = y.astype(jnp.float32)
     u = jnp.log(jnp.abs(y)) * (1.0 / (POWER * LN2)) + FLOOR / POWER
-    return jnp.where(y != 0.0, jnp.exp2(jnp.where(y < 0.0, -u, u) + MID), 0.0)
+    return jnp.exp2(jnp.where(y < 0.0, -u, u) + MID)
 
 
 def kernel(chunks, slots, rows, columns, live, blocks, slab, e_out, mass_out,
@@ -78,7 +79,7 @@
 
     def remote(kind, k, src, dst, dev):
         if kind < WIDE:
-            sems = wide_send.at[kind, k], wide_recv.at[kind, k]
+            sems = wide_send.at[kind - CORE, k], wide_recv.at[kind, k]
         else:
             sems = send.at[kind - WIDE, lax.rem(k, TURNS)], recv.at[kind - WIDE, lax.rem(k, TURNS)]
         return pltpu.make_async_remote_copy(
@@ -139,8 +140,13 @@
     def m2a_copies(k):
         return pair_copies(M2AP, k, m2as, m2ar)
 
+    def m2b_part(k, n):
+        slot = lax.rem(k, 2)
+        return [remote(M2BP + 3 * n, k, m2bs.at[slot, 0, n], m2br.at[k, 0, n], dev_zp),
+                remote(M2BM + 3 * n, k, m2bs.at[slot, 1, n], m2br.at[k, 1, n], dev_zm)]
+
     def m2b_copies(k):
-        return pair_copies(M2BP, k, m2bs, m2br)
+        return m2b_part(k, 0) + m2b_part(k, 1) + m2b_part(k, 2)
 
     def x1_copy(k):
         return remote(X1, k, x1s.at[lax.rem(k, 2)], x1r.at[k], dev_x2)
@@ -151,8 +157,11 @@
     def eb_copies(k):
         return pair_copies(EBP, k, ebs, ebr)
 
-    def mx_copy(k):
-        return remote(MX, k, mxs.at[lax.rem(k, 2)], mxr.at[k], dev_x2)
+    def mx_part(k, n):
+        return remote(MX + 3 * n, k, mxs.at[lax.rem(k, 2), n], mxr.at[k, n], dev_x2)
+
+    def mx_copies(k):
+        return [mx_part(k, n) for n in range(SPLIT)]
 
     def outc_copy(k):
         return remote(OUTC, k, fin.at[lax.rem(k, 2), pl.ds((1 - q) * 2, 2)], e_out.at[:, :, cols(q, k)], dev_core)
@@ -194,7 +203,7 @@
 
     def list_slots():
         number = lax.broadcasted_iota(jnp.int32, (1, slots), 1)
-        key = jnp.where(number < live[0, 0], rows[...] - i * 32, 32)
+        key = jnp.where(number < live[...], rows[...] - i * 32, 32)
         place = lax.shift_right_logical(columns[...], 5) * 4 + q * 2 + (columns[...] & 1)
         meta[...] = jnp.full((8, LANES), 64, jnp.int32)
 
@@ -392,13 +401,10 @@
         arrived(M1P, k, m1r.at[k, 0], dev_zm)
         arrived(M1M, k, m1r.at[k, 1], dev_zp)
 
-        def pack(n, _):
+        for n in range(SPLIT):
             for d in range(2):
                 m2bs[slot, d, n] = encode(t_buf[d, n] + decode(m1r[k, d, n]))
-            return 0
-
-        lax.fori_loop(0, 3, pack, 0)
-        start(m2b_copies(k))
+            start(m2b_part(k, n))
 
         arrived(X1, k, x1r.at[k], dev_x2)
 
@@ -419,24 +425,19 @@
 
         @pl.when(k >= 2)
         def _():
-            mx_copy(k - 2).wait_send()
-            for copy in eb_copies(k - 2):
-                copy.wait_send()
+            sent(mx_copies(k - 2) + eb_copies(k - 2))
 
         arrived(M2AP, k, m2ar.at[k, 0], dev_zm)
         arrived(M2AM, k, m2ar.at[k, 1], dev_zp)
-        arrived(M2BP, k, m2br.at[k, 0], dev_zm)
-        arrived(M2BM, k, m2br.at[k, 1], dev_zp)
 
         def total(h, n):
             return s_buf[keep_slot, h, n] + (decode(m2br[k, h, n]) + decode(m2ar[k, 1 - h, n]))
 
-        def pack(n, _):
+        for n in range(SPLIT):
+            arrived(M2BP + 3 * n, k, m2br.at[k, 0, n], dev_zm)
+            arrived(M2BM + 3 * n, k, m2br.at[k, 1, n], dev_zp)
             mxs[slot, n] = encode(total(1 - xh, n))
-            return 0
-
-        lax.fori_loop(0, 3, pack, 0)
-        mx_copy(k).start()
+            mx_part(k, n).start()
 
         arrived(EAP, k, ear.at[k, 0], dev_zm)
         arrived(EAM, k, ear.at[k, 1], dev_zp)
@@ -469,14 +470,12 @@
         fin[slot, 3, HIGH] = high
         acc = jnp.sum((low * low + high * high).reshape(-1, 8, LANES), axis=0)
 
-        arrived(MX, k, mxr.at[k], dev_x2)
-
-        def add(n, acc):
+        for n in range(SPLIT):
+            arrived(MX + 3 * n, k, mxr.at[k, n], dev_x2)
             value = s_buf[keep_slot, xh, n] + decode(mxr[k, n])
             fin[slot, n] = value
-            return acc + jnp.sum((value * value).reshape(-1, 8, LANES), axis=0)
-
-        acc = lax.fori_loop(0, 3, add, acc)
+            acc = acc + jnp.sum((value * value).reshape(-1, 8, LANES), axis=0)
+
         outc_copy(k).start()
         outl_copy(k).start()
         ms[0] = jnp.where(lane_row == k, jnp.sum(acc, axis=0, keepdims=True), ms[0])
@@ -527,6 +526,36 @@
         src_ref=ms.at[0], dst_ref=mr_plane.at[n], send_sem=mass_send.at[n], recv_sem=mass_recv.at[n],
         device_id=dev, device_id_type=MESH) for n, dev in enumerate(plane)]
     start(copies)
+
+    a_remote().wait_send()
+
+    def drain(k, _):
+        core_copy(k).wait_send()
+        arrived(OUTC, k, e_out.at[:, :, cols(1 - q, k)], dev_core)
+        return 0
+
+    lax.fori_loop(0, chunks, drain, 0)
+
+    def drain_pieces(k, _):
+        sent([x_copy(k)] + y_copies(k) + fwd_copies(k) + fwdx_copies(k))
+        by_fork(k, lambda forked: sent(yx_copies(k, forked) + (fork_copies(k) if forked else [])))
+        return 0
+
+    lax.fori_loop(chunks - TURNS, chunks, drain_pieces, 0)
+
+    sent(m1_copies(chunks - 2))
+
+    def drain_last(k, _):
+        for copy in m2a_copies(k) + m2b_copies(k) + ea_copies(k) + eb_copies(k):
+            copy.wait_send()
+        x1_copy(k).wait_send()
+        sent(mx_copies(k))
+        outc_copy(k).wait_send()
+        outl_copy(k).wait()
+        return 0
+
+    lax.fori_loop(chunks - 2, chunks, drain_last, 0)
+
     for copy in copies:
         copy.wait()
     ms[1] = ms[0] + jnp.sum(mr_plane[...], axis=0)
@@ -539,35 +568,6 @@
     mass_out[q] = ms[1] + jnp.sum(mr_line[0:3], axis=0)
     mass_out[1 - q] = jnp.sum(mr_line[3:7], axis=0)
 
-    a_remote().wait_send()
-
-    def drain(k, _):
-        core_copy(k).wait_send()
-        arrived(OUTC, k, e_out.at[:, :, cols(1 - q, k)], dev_core)
-        return 0
-
-    lax.fori_loop(0, chunks, drain, 0)
-
-    def drain_pieces(k, _):
-        sent([x_copy(k)] + y_copies(k) + fwd_copies(k) + fwdx_copies(k))
-        by_fork(k, lambda forked: sent(yx_copies(k, forked) + (fork_copies(k) if forked else [])))
-        return 0
-
-    lax.fori_loop(chunks - TURNS, chunks, drain_pieces, 0)
-
-    sent(m1_copies(chunks - 2))
-
-    def drain_last(k, _):
-        for copy in m2a_copies(k) + m2b_copies(k) + ea_copies(k) + eb_copies(k):
-            copy.wait_send()
-        x1_copy(k).wait_send()
-        mx_copy(k).wait_send()
-        outc_copy(k).wait_send()
-        outl_copy(k).wait()
-        return 0
-
-    lax.fori_loop(chunks - 2, chunks, drain_last, 0)
-
 
 def body(blocks, block_rows, block_cols, live_count, slab):
     slots, bs = blocks.shape[2], blocks.shape[3]
@@ -580,7 +580,7 @@
         functools.partial(kernel, chunks, slots),
         out_shape=(jax.ShapeDtypeStruct((2, bs, width), f32), jax.ShapeDtypeStruct((2, chunks, LANES), f32)),
         in_specs=[pl.BlockSpec(memory_space=pltpu.VMEM), pl.BlockSpec(memory_space=pltpu.VMEM),
-                  pl.BlockSpec(memory_space=pltpu.SMEM),
+                  pl.BlockSpec(memory_space=pltpu.VMEM),
                   pl.BlockSpec(memory_space=pl.ANY), pl.BlockSpec(memory_space=pl.ANY)],
         out_specs=(pl.BlockSpec(memory_space=pl.ANY), pl.BlockSpec(memory_space=pltpu.VMEM)),
         scratch_shapes=[
@@ -602,7 +602,7 @@
             vm((2, chunks, LANES), f32), vm((15, chunks, LANES), f32), vm((7, chunks, LANES), f32),
             vm((8, LANES), jnp.int32), vm((8, LANES), jnp.int32), vm((8, LANES), jnp.int32), vm((8, LANES), f32),
             pltpu.SMEM((8, LANES), jnp.int32), pltpu.SMEM((8, LANES), f32),
-            pltpu.SemaphoreType.DMA((WIDE, chunks)), pltpu.SemaphoreType.DMA((WIDE, chunks)),
+            pltpu.SemaphoreType.DMA((2, chunks)), pltpu.SemaphoreType.DMA((WIDE, chunks)),
             pltpu.SemaphoreType.DMA((KINDS - WIDE, TURNS)), pltpu.SemaphoreType.DMA((KINDS - WIDE, TURNS)),
             pltpu.SemaphoreType.DMA((1,)), pltpu.SemaphoreType.DMA((2,)),
             pltpu.SemaphoreType.DMA((22,)), pltpu.SemaphoreType.DMA((22,)),

time: 192 us -> 189 us (0.984)
  Pallas kernels: 185 us -> 183 us
    pallas_call x1, Pallas kernels: 185 us -> 183 us  [body(): pl.pallas_call(functools.partial(kernel, chunks, slots), out_shape=(jax.S...]
where the time goes in v5:
time: 189 us
  Pallas kernels  183 us (97%)
  other arithmetic  5.67 us (3%)
    pallas_call x1, Pallas kernels, body(): pl.pallas_call(functools.partial(kernel, chunks, slots), out_shape=(jax.S...  183 us
    mul x1, other arithmetic, body(): return (e * e * scale).reshape(depth, width)  4.97 us

profile of v5, /device:TPU:1, one launch (start us, length us, event | category | flops | bytes accessed | tf_op | source)
XLA Modules:
  0.0 189.1 jit_solution(4792397118574724202)
XLA Ops:
  0.7 182.8 %shard_map.55 = (f32[2,256,2048]{2,1,0:T(8,128)}, f32[2,8,128]{2,1,0:T(8,128)}) custom-call(s32[1,24]{1,0:T(1,128)} %bitcast.9, s32[1,24]{1,0:T(1,128)} %bitcast.10, s32[1,1]{1,0:T(1,128)S(6)} %copy.6.live, bf16[24,256,256]{2,1,0:T(8,128)(2,1)} %bitcast.7, bf16[2,256,2048]{2,1,0:T(8,128)(2,1)} %bitcast.8), custom_call_target="tpu_custom_call" | custom-call | flops 6442450944 | bytes 16777216 | tf_op jit(solution)/shard_map/pallas_call | solution.py:579
  183.5 0.7 divide_bitcast_fusion
  184.2 5.0 %multiply_multiply_fusion = f32[2,256,2048]{2,1,0:T(8,128)} fusion(f32[2,256,2048]{2,1,0:T(8,128)} %get-tuple-element.7, f32[2048]{0:T(1024)S(1)} %divide_bitcast_fusion), kind=kLoop, calls=%fused_computation | loop fusion | flops 2097152 | bytes 8396800 | tf_op jit(solution)/shard_map/mul | solution.py:617

commit v6 on v5

--- a/solution.py
+++ b/solution.py
@@ -11,7 +11,7 @@
 LOW, HIGH = pl.ds(0, 128), pl.ds(128, 128)
 
 LANES = 128
-FORKED = 4
+FORK_TWO, FORK_ONE = 2, 4
 MID, POWER, FLOOR = 6.0, 26.0, 117.0
 LN2 = 0.6931471805599453
 
@@ -107,21 +107,25 @@
         return [piece_copy(YPA, k, i, dev_yp), piece_copy(YMA, k, i, dev_ym)]
 
     def yx_copies(k, forked):
-        if forked:
-            return [piece_copy(YPB, k, xi, dev_yp, 0, 3), piece_copy(YMB, k, xi, dev_ym, 1, 3)]
-        return [piece_copy(YPB, k, xi, dev_yp), piece_copy(YMB, k, xi, dev_ym)]
-
-    def fork_copies(k):
-        return [piece_copy(XF0, k, ym, dev_x, 3, 1), piece_copy(XF1, k, yp, dev_x, 0, 1)]
+        return [piece_copy(YPB, k, xi, dev_yp, 0, 4 - forked), piece_copy(YMB, k, xi, dev_ym, forked, 4 - forked)]
+
+    def fork_copies(k, forked):
+        if not forked:
+            return []
+        return [piece_copy(XF0, k, ym, dev_x, 4 - forked, forked), piece_copy(XF1, k, yp, dev_x, 0, forked)]
 
     def by_fork(k, act):
-        @pl.when(k < FORKED)
-        def _():
-            act(True)
-
-        @pl.when(k >= FORKED)
-        def _():
-            act(False)
+        @pl.when(k < FORK_TWO)
+        def _():
+            act(2)
+
+        @pl.when((k >= FORK_TWO) & (k < FORK_ONE))
+        def _():
+            act(1)
+
+        @pl.when(k >= FORK_ONE)
+        def _():
+            act(0)
 
     def fwd_copies(k):
         return [piece_copy(YPC, k, ym, dev_yp, 0, 2), piece_copy(YMC, k, yp, dev_ym, 2, 2)]
@@ -283,22 +287,16 @@
         @pl.when(k >= TURNS)
         def _():
             sent(fwd_copies(k - TURNS) + fwdx_copies(k - TURNS))
-
-            @pl.when(k - TURNS < FORKED)
-            def _():
-                sent(fork_copies(k - TURNS))
+            by_fork(k - TURNS, lambda forked: sent(fork_copies(k - TURNS, forked)))
 
         arrived(YPA, k, piece(k, ym), dev_ym)
         arrived(YMA, k, piece(k, yp), dev_yp)
         start(fwd_copies(k))
 
-        @pl.when(k < FORKED)
-        def _():
-            start(fork_copies(k))
-
         def rest(forked):
-            arrived(YPB, k, piece(k, xym, 0, 3 if forked else 4), dev_ym)
-            arrived(YMB, k, piece(k, xyp, *((1, 3) if forked else (0, 4))), dev_yp)
+            start(fork_copies(k, forked))
+            arrived(YPB, k, piece(k, xym, 0, 4 - forked), dev_ym)
+            arrived(YMB, k, piece(k, xyp, forked, 4 - forked), dev_yp)
 
         by_fork(k, rest)
         start(fwdx_copies(k))
@@ -312,10 +310,12 @@
         arrived(YPD, k, piece(k, xy2, 0, 2), dev_ym)
         arrived(YMD, k, piece(k, xy2, 2, 2), dev_yp)
 
-        @pl.when(k < FORKED)
-        def _():
-            arrived(XF0, k, piece(k, xym, 3, 1), dev_x)
-            arrived(XF1, k, piece(k, xyp, 0, 1), dev_x)
+        def by_x(forked):
+            if forked:
+                arrived(XF0, k, piece(k, xym, 4 - forked, forked), dev_x)
+                arrived(XF1, k, piece(k, xyp, 0, forked), dev_x)
+
+        by_fork(k, by_x)
 
         move = pltpu.make_async_copy(b_buf.at[k], b_cmp, cmp_sem.at[0])
         move.start()
@@ -538,7 +538,7 @@
 
     def drain_pieces(k, _):
         sent([x_copy(k)] + y_copies(k) + fwd_copies(k) + fwdx_copies(k))
-        by_fork(k, lambda forked: sent(yx_copies(k, forked) + (fork_copies(k) if forked else [])))
+        by_fork(k, lambda forked: sent(yx_copies(k, forked) + fork_copies(k, forked)))
         return 0
 
     lax.fori_loop(chunks - TURNS, chunks, drain_pieces, 0)

time: 189 us -> 187 us (0.989)
  Pallas kernels: 183 us -> 181 us
    pallas_call x1, Pallas kernels: 183 us -> 181 us  [body(): pl.pallas_call(functools.partial(kernel, chunks, slots), out_shape=(jax.S...]
where the time goes in v6:
time: 187 us
  Pallas kernels  181 us (97%)
  other arithmetic  5.67 us (3%)
    pallas_call x1, Pallas kernels, body(): pl.pallas_call(functools.partial(kernel, chunks, slots), out_shape=(jax.S...  181 us
    mul x1, other arithmetic, body(): return (e * e * scale).reshape(depth, width)  4.97 us

profile of v6, /device:TPU:1, one launch (start us, length us, event | category | flops | bytes accessed | tf_op | source)
XLA Modules:
  0.0 187.2 jit_solution(17080017982421982271)
XLA Ops:
  0.7 180.9 %shard_map.55 = (f32[2,256,2048]{2,1,0:T(8,128)}, f32[2,8,128]{2,1,0:T(8,128)}) custom-call(s32[1,24]{1,0:T(1,128)} %bitcast.9, s32[1,24]{1,0:T(1,128)} %bitcast.10, s32[1,1]{1,0:T(1,128)S(6)} %copy.6.live, bf16[24,256,256]{2,1,0:T(8,128)(2,1)} %bitcast.7, bf16[2,256,2048]{2,1,0:T(8,128)(2,1)} %bitcast.8), custom_call_target="tpu_custom_call" | custom-call | flops 6442450944 | bytes 16777216 | tf_op jit(solution)/shard_map/pallas_call | solution.py:579
  181.5 0.7 divide_bitcast_fusion
  182.3 5.0 %multiply_multiply_fusion = f32[2,256,2048]{2,1,0:T(8,128)} fusion(f32[2,256,2048]{2,1,0:T(8,128)} %get-tuple-element.7, f32[2048]{0:T(1024)S(1)} %divide_bitcast_fusion), kind=kLoop, calls=%fused_computation | loop fusion | flops 2097152 | bytes 8396800 | tf_op jit(solution)/shard_map/mul | solution.py:617

commit v7 on v6

--- a/solution.py
+++ b/solution.py
@@ -334,7 +334,7 @@
                 a_buf[tab[0, p]], b_cmp[tab[1, p]], preferred_element_type=jnp.float32)
             return 0
 
-        lax.fori_loop(0, 2 * slots, product, 0, unroll=8)
+        lax.fori_loop(0, 2 * slots, product, 0, unroll=16)
 
         slot = lax.rem(k, 2)
 
@@ -365,10 +365,6 @@
             return 0
 
         lax.fori_loop(0, 3, pack2, 0)
-
-        @pl.when(k == chunks - 1)
-        def _():
-            sent(m1_copies(k))
 
         start(m2a_copies(k))
 
@@ -544,6 +540,7 @@
     lax.fori_loop(chunks - TURNS, chunks, drain_pieces, 0)
 
     sent(m1_copies(chunks - 2))
+    sent(m1_copies(chunks - 1))
 
     def drain_last(k, _):
         for copy in m2a_copies(k) + m2b_copies(k) + ea_copies(k) + eb_copies(k):

time: 187 us -> 187 us (level)
  no operation moved by 1% of the time
where the time goes in v7:
time: 187 us
  Pallas kernels  180 us (96%)
  other arithmetic  5.67 us (3%)
    pallas_call x1, Pallas kernels, body(): pl.pallas_call(functools.partial(kernel, chunks, slots), out_shape=(jax.S...  180 us
    mul x1, other arithmetic, body(): return (e * e * scale).reshape(depth, width)  4.97 us

profile of v7, /device:TPU:1, one launch (start us, length us, event | category | flops | bytes accessed | tf_op | source)
XLA Modules:
  0.0 186.5 jit_solution(10888155862573917520)
XLA Ops:
  0.7 180.2 %shard_map.55 = (f32[2,256,2048]{2,1,0:T(8,128)}, f32[2,8,128]{2,1,0:T(8,128)}) custom-call(s32[1,24]{1,0:T(1,128)} %bitcast.9, s32[1,24]{1,0:T(1,128)} %bitcast.10, s32[1,1]{1,0:T(1,128)S(6)} %copy.6.live, bf16[24,256,256]{2,1,0:T(8,128)(2,1)} %bitcast.7, bf16[2,256,2048]{2,1,0:T(8,128)(2,1)} %bitcast.8), custom_call_target="tpu_custom_call" | custom-call | flops 6442450944 | bytes 16777216 | tf_op jit(solution)/shard_map/pallas_call | solution.py:576
  180.9 0.7 divide_bitcast_fusion
  181.6 5.0 %multiply_multiply_fusion = f32[2,256,2048]{2,1,0:T(8,128)} fusion(f32[2,256,2048]{2,1,0:T(8,128)} %get-tuple-element.7, f32[2048]{0:T(1024)S(1)} %divide_bitcast_fusion), kind=kLoop, calls=%fused_computation | loop fusion | flops 2097152 | bytes 8396800 | tf_op jit(solution)/shard_map/mul | solution.py:614
